TPU v7x, 32 devices: a whole 2x2x4 slice. The times are simulated.
32 devices in a mesh: tiles: 16 (over z, y, x), rep: 2 (over core).
Axes of the slice: x: 2, y: 2, z: 4, core: 2. Of those that a mesh axis runs over, the one named last changes fastest.
Arguments:
- members: bfloat16 [512, 80, 256], P(('tiles', 'rep')), may hold values from -1350 to 1350
- initial: bfloat16 [512, 32, 256], P(('tiles', 'rep')), may hold values from -6 to 6
- wet_counts: int32 [512], P(('tiles', 'rep')), may hold values from 1 to 256, as said below
- tile_coords: int32 [512, 2], P(('tiles', 'rep')), may hold values from 0 to 63, as said below
- neighbours: int32 [512, 9], P(('tiles', 'rep')), may hold values from -1 to 511, as said below
Outputs:
- leading: float32 [512, 32, 256], P(('tiles', 'rep'))
Inputs may be any that keep to these rules, and one draw needn't show every extreme that they name: `wet_counts`: each tile's count of wet points; some tiles are all wet. `tile_coords`: tiles form a strip of columns of 8 consecutive tiles; the first entry is the column, consecutive columns are offset by at most one tile in the second entry. `neighbours`: each tile lists, in increasing order and followed by -1 padding, every tile whose two entries of tile_coords differ from its own by at most one, itself included; the list is symmetric.
All inputs are finite; a program needn't handle non-finite values.
Results may differ from a plain program's by a relative error of at most 0.00065.
The roundings to bfloat16 on the way count: a program that leaves them out, or rounds other values in their place, can miss the bound.
Values may be sent and summed in bfloat16 or wider, within the bound.
A program may use at most 128 MiB of HBM per device.

v0:
```python
import jax
import jax.numpy as jnp
from jax import lax
from jax.sharding import PartitionSpec as P

TILE_SIDE = 16
COLW = 8
ITERS = 2


def from_behind(shard, axis, by):
    length = lax.axis_size(axis)
    pairs = [(i, i + by) for i in range(length) if 0 <= i + by < length]
    return lax.ppermute(shard, axis, pairs)


def gaspari(distance):
    scaled = distance / (0.5 * TILE_SIDE)
    clamped = jnp.maximum(scaled, 1.0)
    inner_part = (
        ((-0.25 * scaled + 0.5) * scaled + 0.625) * scaled - 5.0 / 3.0
    ) * scaled * scaled + 1.0
    outer_part = (
        ((((scaled / 12.0 - 0.5) * scaled + 0.625) * scaled + 5.0 / 3.0) * scaled - 5.0) * scaled
        + 4.0
        - 2.0 / (3.0 * clamped)
    )
    return jnp.where(scaled <= 1.0, inner_part, jnp.where(scaled <= 2.0, outer_part, 0.0))


def distances(place_one, place_two):
    points = jnp.arange(TILE_SIDE * TILE_SIDE, dtype=jnp.int32)
    across = points // TILE_SIDE
    along_row = points % TILE_SIDE
    row_one = place_one[..., 0:1] * TILE_SIDE + across
    col_one = place_one[..., 1:2] * TILE_SIDE + along_row
    row_two = place_two[..., 0:1] * TILE_SIDE + across
    col_two = place_two[..., 1:2] * TILE_SIDE + along_row
    delta_row = (row_one[..., :, None] - row_two[..., None, :]).astype(jnp.float32)
    delta_col = (col_one[..., :, None] - col_two[..., None, :]).astype(jnp.float32)
    return jnp.sqrt(delta_row * delta_row + delta_col * delta_col)


def tapered(rows_one, place_one, rows_two, place_two):
    product = jnp.einsum("hmi,hmj->hij", rows_one, rows_two, preferred_element_type=jnp.float32)
    weight = gaspari(distances(place_one, place_two))
    return (product * weight / (rows_one.shape[1] - 1.0)).astype(jnp.bfloat16)


def member_window(own_rows, own_place, lowest, reach_count):
    rows_list = []
    place_list = []
    for start_offset in range(lowest, reach_count + 1):
        if start_offset == 0:
            rows_list.append(own_rows)
            place_list.append(own_place)
        else:
            moved_rows, moved_place = from_behind(
                (own_rows, own_place), ("tiles", "rep"), -start_offset
            )
            rows_list.append(moved_rows)
            place_list.append(moved_place)
    return (jnp.concatenate(rows_list, 0), jnp.concatenate(place_list, 0))


def iterate_window(current, lowest, reach_count):
    iter_list = []
    for start_offset in range(lowest, reach_count + 1):
        if start_offset == 0:
            iter_list.append(current)
        else:
            iter_list.append(from_behind(current, ("tiles", "rep"), -start_offset))
    return jnp.concatenate(iter_list, 0)


def form_blocks(own_rows, own_place, listed, window_rows, window_place, window_base):
    window_at = jnp.clip(listed - window_base, 0, window_rows.shape[0] - 1)
    slot_at = jnp.transpose(window_at)

    def one_slot(at_here):
        return tapered(own_rows, own_place, window_rows[at_here], window_place[at_here])

    return (slot_at, lax.map(one_slot, slot_at))


def both_sides(listed, slot_at, blocks, window_iter, rank_count, points):
    tiles_here = listed.shape[0]

    def advance(totals, inputs):
        column, at_here, block_here = inputs
        contrib = jnp.einsum(
            "hkj,hij->hki", window_iter[at_here], block_here, preferred_element_type=jnp.float32
        )
        contrib = jnp.where((column >= 0)[:, None, None], contrib, 0.0)
        return (totals + contrib, None)

    empty = jnp.zeros((tiles_here, rank_count, points), jnp.float32)
    totals, unused = lax.scan(advance, empty, (jnp.transpose(listed), slot_at, blocks))
    return totals


def orthonormal(applied_product, total_points):
    tile_gram = jnp.einsum(
        "brg,bsg->rs",
        applied_product,
        applied_product,
        precision=lax.Precision.HIGHEST,
        preferred_element_type=jnp.float32,
    )
    summed_gram = lax.psum(tile_gram, ("tiles", "rep")) / total_points
    factor = jnp.linalg.cholesky(summed_gram)
    inverse_factor = jax.scipy.linalg.solve_triangular(
        factor, jnp.eye(summed_gram.shape[0], dtype=jnp.float32), lower=True
    )
    return jnp.einsum(
        "fy,ryc->rfc",
        inverse_factor,
        applied_product,
        precision=lax.Precision.HIGHEST,
        preferred_element_type=jnp.float32,
    )


def local(members, initial, wet_counts, tile_coords, neighbours):
    tiles_here = members.shape[0]
    points = members.shape[2]
    rank_count = initial.shape[1]
    reach_count = (COLW + 2 + tiles_here - 1) // tiles_here
    first_tile = lax.axis_index(("tiles", "rep")) * tiles_here
    total_points = float(tiles_here * lax.axis_size(("tiles", "rep")) * points)
    wet_mask = jnp.arange(points, dtype=jnp.int32)[None, :] < wet_counts[:, None]
    own_rows = jnp.where(wet_mask[:, None, :], members, jnp.zeros_like(members))
    lowest = -reach_count
    window_rows, window_place = member_window(own_rows, tile_coords, lowest, reach_count)
    slot_at, blocks = form_blocks(
        own_rows,
        tile_coords,
        neighbours,
        window_rows,
        window_place,
        first_tile + lowest * tiles_here,
    )
    current = initial
    fresh = jnp.zeros(initial.shape, jnp.float32)
    for sweep_index in range(ITERS):
        window_iter = iterate_window(current, lowest, reach_count)
        applied_product = both_sides(neighbours, slot_at, blocks, window_iter, rank_count, points)
        fresh = orthonormal(applied_product, total_points)
        current = fresh.astype(jnp.bfloat16)
    return fresh


def solution(mesh):
    in_specs = (
        P(("tiles", "rep"), None, None),
        P(("tiles", "rep"), None, None),
        P(("tiles", "rep")),
        P(("tiles", "rep"), None),
        P(("tiles", "rep"), None),
    )
    out_specs = P(("tiles", "rep"), None, None)
    return jax.shard_map(local, mesh=mesh, in_specs=in_specs, out_specs=out_specs, check_vma=False)
```

profile of v0, /device:TPU:0, one launch (start us, length us, event | category | flops | bytes accessed | tf_op | source)
XLA Modules:
  0.0 344.9 jit_solution(14677899201445447853)
XLA Ops:
  6.4 5.1 %collective-permute-start = (bf16[16,32,256]{2,1,0:T(8,128)(2,1)}, bf16[16,32,256]{2,1,0:T(8,128)(2,1)S(1)}, u32[]{:S(2)}, u32[]{:S(2)}) collective-permute-start(bf16[16,32,256]{2,1,0:T(8,128)(2,1)} %param.15), channel_id=1, source_target_pairs={{0,1},{1,2},{2,3},{3,4},{4,5},{5,6},{6,7},{7,8},{8,9},{9,10},{10,1... | collective-permute-start | bytes 786440 | tf_op jit(solution)/shard_map/ppermute | solution.py:14
  12.8 4.3 %collective-permute-start.4 = (s32[16,2]{0,1:T(2,128)}, s32[16,2]{0,1:T(2,128)S(1)}, u32[]{:S(2)}, u32[]{:S(2)}) collective-permute-start(s32[16,2]{0,1:T(2,128)} %param.17), channel_id=1, source_target_pairs={{0,1},{1,2},{2,3},{3,4},{4,5},{5,6},{6,7},{7,8},{8,9},{9,10},{10,1... | collective-permute-start | bytes 392 | tf_op jit(solution)/shard_map/ppermute | solution.py:14
  20.0 10.9 %collective-permute-done.5 = s32[16,2]{0,1:T(2,128)S(1)} collective-permute-done((s32[16,2]{0,1:T(2,128)}, s32[16,2]{0,1:T(2,128)S(1)}, u32[]{:S(2)}, u32[]{:S(2)}) %collective-permute-start.5) | collective-permute-done | bytes 160 | tf_op jit(solution)/shard_map/ppermute | solution.py:14
  35.4 146.8 %while.34 = (s32[]{:T(128)}, bf16[9,16,256,256]{3,2,1,0:T(8,128)(2,1)}, s32[9,16]{1,0:T(8,128)S(1)}, bf16[48,80,256]{2,1,0:T(8,128)(2,1)}, bf16[16,80,256]{2,1,0...) while((s32[]{:T(128)}, bf16[9,16,256,256]{3,2,1,0:T(8,128)(2,1)}, ...), condition=%wide.region_1.2_spmd, body=%wide.region_0.1_spmd.sunk | while | flops 207639152 | bytes 13248409 | solution.py:83
  38.6 8.8 %fusion.74 = bf16[1,16,256,256]{2,3,1,0:T(8,128)(2,1)} fusion(s32[16,256]{1,0:T(8,128)S(1)} %get-tuple-element.435, s32[16,256]{1,0:T(8,128)S(1)} %get-tuple-element.436, s32[16,256]{1,0:T(8,128)S(1)} %get-tuple-element.437, s32[16,256]{1,0:T(8,128)S(1)} %get-tuple-element.438, bf16[16,80,256]{2,1,0:T(8,128)(2,1)S(1)} %gather_fusion.1, ...), kind=kOutput, calls=%fused_computation.40.clone.1 | convolution fusion | flops 207618048 | bytes 3473408 | tf_op jit(solution)/shard_map/while/body/eval_jaxpr/hmi,hmj->hij/dot_general | solution.py:45
  47.4 2.8 copy.47
  54.9 8.8 %fusion.74 = bf16[1,16,256,256]{2,3,1,0:T(8,128)(2,1)} fusion(s32[16,256]{1,0:T(8,128)S(1)} %get-tuple-element.435, s32[16,256]{1,0:T(8,128)S(1)} %get-tuple-element.436, s32[16,256]{1,0:T(8,128)S(1)} %get-tuple-element.437, s32[16,256]{1,0:T(8,128)S(1)} %get-tuple-element.438, bf16[16,80,256]{2,1,0:T(8,128)(2,1)S(1)} %gather_fusion.1, ...), kind=kOutput, calls=%fused_computation.40.clone.1 | convolution fusion | flops 207618048 | bytes 3473408 | tf_op jit(solution)/shard_map/while/body/eval_jaxpr/hmi,hmj->hij/dot_general | solution.py:45
  71.2 8.8 %fusion.74 = bf16[1,16,256,256]{2,3,1,0:T(8,128)(2,1)} fusion(s32[16,256]{1,0:T(8,128)S(1)} %get-tuple-element.435, s32[16,256]{1,0:T(8,128)S(1)} %get-tuple-element.436, s32[16,256]{1,0:T(8,128)S(1)} %get-tuple-element.437, s32[16,256]{1,0:T(8,128)S(1)} %get-tuple-element.438, bf16[16,80,256]{2,1,0:T(8,128)(2,1)S(1)} %gather_fusion.1, ...), kind=kOutput, calls=%fused_computation.40.clone.1 | convolution fusion | flops 207618048 | bytes 3473408 | tf_op jit(solution)/shard_map/while/body/eval_jaxpr/hmi,hmj->hij/dot_general | solution.py:45
  87.5 8.8 %fusion.74 = bf16[1,16,256,256]{2,3,1,0:T(8,128)(2,1)} fusion(s32[16,256]{1,0:T(8,128)S(1)} %get-tuple-element.435, s32[16,256]{1,0:T(8,128)S(1)} %get-tuple-element.436, s32[16,256]{1,0:T(8,128)S(1)} %get-tuple-element.437, s32[16,256]{1,0:T(8,128)S(1)} %get-tuple-element.438, bf16[16,80,256]{2,1,0:T(8,128)(2,1)S(1)} %gather_fusion.1, ...), kind=kOutput, calls=%fused_computation.40.clone.1 | convolution fusion | flops 207618048 | bytes 3473408 | tf_op jit(solution)/shard_map/while/body/eval_jaxpr/hmi,hmj->hij/dot_general | solution.py:45
  96.3 2.8 copy.47
  103.8 8.8 %fusion.74 = bf16[1,16,256,256]{2,3,1,0:T(8,128)(2,1)} fusion(s32[16,256]{1,0:T(8,128)S(1)} %get-tuple-element.435, s32[16,256]{1,0:T(8,128)S(1)} %get-tuple-element.436, s32[16,256]{1,0:T(8,128)S(1)} %get-tuple-element.437, s32[16,256]{1,0:T(8,128)S(1)} %get-tuple-element.438, bf16[16,80,256]{2,1,0:T(8,128)(2,1)S(1)} %gather_fusion.1, ...), kind=kOutput, calls=%fused_computation.40.clone.1 | convolution fusion | flops 207618048 | bytes 3473408 | tf_op jit(solution)/shard_map/while/body/eval_jaxpr/hmi,hmj->hij/dot_general | solution.py:45
  120.2 8.8 %fusion.74 = bf16[1,16,256,256]{2,3,1,0:T(8,128)(2,1)} fusion(s32[16,256]{1,0:T(8,128)S(1)} %get-tuple-element.435, s32[16,256]{1,0:T(8,128)S(1)} %get-tuple-element.436, s32[16,256]{1,0:T(8,128)S(1)} %get-tuple-element.437, s32[16,256]{1,0:T(8,128)S(1)} %get-tuple-element.438, bf16[16,80,256]{2,1,0:T(8,128)(2,1)S(1)} %gather_fusion.1, ...), kind=kOutput, calls=%fused_computation.40.clone.1 | convolution fusion | flops 207618048 | bytes 3473408 | tf_op jit(solution)/shard_map/while/body/eval_jaxpr/hmi,hmj->hij/dot_general | solution.py:45
  128.9 2.8 copy.47
  136.4 8.8 %fusion.74 = bf16[1,16,256,256]{2,3,1,0:T(8,128)(2,1)} fusion(s32[16,256]{1,0:T(8,128)S(1)} %get-tuple-element.435, s32[16,256]{1,0:T(8,128)S(1)} %get-tuple-element.436, s32[16,256]{1,0:T(8,128)S(1)} %get-tuple-element.437, s32[16,256]{1,0:T(8,128)S(1)} %get-tuple-element.438, bf16[16,80,256]{2,1,0:T(8,128)(2,1)S(1)} %gather_fusion.1, ...), kind=kOutput, calls=%fused_computation.40.clone.1 | convolution fusion | flops 207618048 | bytes 3473408 | tf_op jit(solution)/shard_map/while/body/eval_jaxpr/hmi,hmj->hij/dot_general | solution.py:45
  152.7 8.8 %fusion.74 = bf16[1,16,256,256]{2,3,1,0:T(8,128)(2,1)} fusion(s32[16,256]{1,0:T(8,128)S(1)} %get-tuple-element.435, s32[16,256]{1,0:T(8,128)S(1)} %get-tuple-element.436, s32[16,256]{1,0:T(8,128)S(1)} %get-tuple-element.437, s32[16,256]{1,0:T(8,128)S(1)} %get-tuple-element.438, bf16[16,80,256]{2,1,0:T(8,128)(2,1)S(1)} %gather_fusion.1, ...), kind=kOutput, calls=%fused_computation.40.clone.1 | convolution fusion | flops 207618048 | bytes 3473408 | tf_op jit(solution)/shard_map/while/body/eval_jaxpr/hmi,hmj->hij/dot_general | solution.py:45
  161.5 2.8 copy.47
  169.0 8.8 %fusion.74 = bf16[1,16,256,256]{2,3,1,0:T(8,128)(2,1)} fusion(s32[16,256]{1,0:T(8,128)S(1)} %get-tuple-element.435, s32[16,256]{1,0:T(8,128)S(1)} %get-tuple-element.436, s32[16,256]{1,0:T(8,128)S(1)} %get-tuple-element.437, s32[16,256]{1,0:T(8,128)S(1)} %get-tuple-element.438, bf16[16,80,256]{2,1,0:T(8,128)(2,1)S(1)} %gather_fusion.1, ...), kind=kOutput, calls=%fused_computation.40.clone.1 | convolution fusion | flops 207618048 | bytes 3473408 | tf_op jit(solution)/shard_map/while/body/eval_jaxpr/hmi,hmj->hij/dot_general | solution.py:45
  182.2 26.7 %while.35 = (s32[]{:T(128)}, f32[16,32,256]{2,1,0:T(8,128)S(1)}, s32[9,16]{1,0:T(8,128)S(1)}, s32[9,16]{1,0:T(8,128)S(1)}, bf16[48,32,256]{2,1,0:T(8,128)(2,1)S(...) while((s32[]{:T(128)}, f32[16,32,256]{2,1,0:T(8,128)S(1)}, ...), condition=%wide.region_3.4_spmd.clone, body=%wide.region_2.3_spmd.clone.sunk | while | flops 67503168 | bytes 3937223 | solution.py:98
  209.5 40.6 %psum.14 = f32[32,32]{0,1:T(8,128)S(1)} all-reduce(f32[32,32]{0,1:T(8,128)S(1)} %convolution_bitcast_fusion.4), channel_id=1, replica_groups=mesh['tiles'=16,'rep'=2] {'tiles','rep'}, use_global_device_ids=true, to_apply=%region_4.5 | all-reduce | flops 1024 | bytes 8192 | tf_op jit(solution)/shard_map/psum | solution.py:110
  250.2 2.9 cholesky.44
  260.3 4.6 %collective-permute-done.7 = bf16[16,32,256]{2,1,0:T(8,128)(2,1)S(1)} collective-permute-done((bf16[16,32,256]{2,1,0:T(8,128)(2,1)S(1)}, bf16[16,32,256]{2,1,0:T(8,128)(2,1)S(1)}, u32[]{:S(2)}, u32[]{:S(2)}) %collective-permute-start.7) | collective-permute-done | bytes 262176 | tf_op jit(solution)/shard_map/ppermute | solution.py:14
  265.0 26.8 %while.36 = (s32[]{:T(128)}, f32[16,32,256]{2,1,0:T(8,128)S(1)}, s32[9,16]{1,0:T(8,128)S(1)}, s32[9,16]{1,0:T(8,128)S(1)}, bf16[48,32,256]{2,1,0:T(8,128)(2,1)S(...) while((s32[]{:T(128)}, f32[16,32,256]{2,1,0:T(8,128)S(1)}, ...), condition=%wide.region_8.11_spmd.clone, body=%wide.region_7.10_spmd.clone.sunk | while | flops 67503168 | bytes 3937223 | solution.py:98
  292.4 44.1 %psum.15 = f32[32,32]{0,1:T(8,128)S(1)} all-reduce(f32[32,32]{0,1:T(8,128)S(1)} %convolution_bitcast_fusion.2), channel_id=1, replica_groups=mesh['tiles'=16,'rep'=2] {'tiles','rep'}, use_global_device_ids=true, to_apply=%region_9.12 | all-reduce | flops 1024 | bytes 8192 | tf_op jit(solution)/shard_map/psum | solution.py:110
  336.6 2.9 cholesky.55
  (230 shorter events, 137.4 us)
Async XLA Ops:
  2.7 30.1 %collective-permute-start.2 = (bf16[16,80,256]{2,1,0:T(8,128)(2,1)}, bf16[16,80,256]{2,1,0:T(8,128)(2,1)S(1)}, u32[]{:S(2)}, u32[]{:S(2)}) collective-permute-start(bf16[16,80,256]{2,1,0:T(8,128)(2,1)} %broadcast_select_fusion), channel_id=1, source_target_pairs={{0,1},{1,2},{2,3},{3,4},{4,5},{5,6},{6,7},{7,8},{8,9},{9,10},{10,1... | collective-permute-start | bytes 1966088 | tf_op jit(solution)/shard_map/ppermute | solution.py:14
  5.1 27.7 %collective-permute-start.3 = (bf16[16,80,256]{2,1,0:T(8,128)(2,1)}, bf16[16,80,256]{2,1,0:T(8,128)(2,1)S(1)}, u32[]{:S(2)}, u32[]{:S(2)}) collective-permute-start(bf16[16,80,256]{2,1,0:T(8,128)(2,1)} %broadcast_select_fusion), channel_id=1, source_target_pairs={{1,0},{2,1},{3,2},{4,3},{5,4},{6,5},{7,6},{8,7},{9,8},{10,9},{11,1... | collective-permute-start | bytes 1966088 | tf_op jit(solution)/shard_map/ppermute | solution.py:14
  6.4 25.3 %collective-permute-start = (bf16[16,32,256]{2,1,0:T(8,128)(2,1)}, bf16[16,32,256]{2,1,0:T(8,128)(2,1)S(1)}, u32[]{:S(2)}, u32[]{:S(2)}) collective-permute-start(bf16[16,32,256]{2,1,0:T(8,128)(2,1)} %param.15), channel_id=1, source_target_pairs={{0,1},{1,2},{2,3},{3,4},{4,5},{5,6},{6,7},{7,8},{8,9},{9,10},{10,1... | collective-permute-start | bytes 786440 | tf_op jit(solution)/shard_map/ppermute | solution.py:14
  11.5 20.2 %collective-permute-start.1 = (bf16[16,32,256]{2,1,0:T(8,128)(2,1)}, bf16[16,32,256]{2,1,0:T(8,128)(2,1)S(1)}, u32[]{:S(2)}, u32[]{:S(2)}) collective-permute-start(bf16[16,32,256]{2,1,0:T(8,128)(2,1)} %param.15), channel_id=1, source_target_pairs={{1,0},{2,1},{3,2},{4,3},{5,4},{6,5},{7,6},{8,7},{9,8},{10,9},{11,1... | collective-permute-start | bytes 786440 | tf_op jit(solution)/shard_map/ppermute | solution.py:14
  12.8 5.8 %collective-permute-start.4 = (s32[16,2]{0,1:T(2,128)}, s32[16,2]{0,1:T(2,128)S(1)}, u32[]{:S(2)}, u32[]{:S(2)}) collective-permute-start(s32[16,2]{0,1:T(2,128)} %param.17), channel_id=1, source_target_pairs={{0,1},{1,2},{2,3},{3,4},{4,5},{5,6},{6,7},{7,8},{8,9},{9,10},{10,1... | collective-permute-start | bytes 392 | tf_op jit(solution)/shard_map/ppermute | solution.py:14
  18.7 12.2 %collective-permute-start.5 = (s32[16,2]{0,1:T(2,128)}, s32[16,2]{0,1:T(2,128)S(1)}, u32[]{:S(2)}, u32[]{:S(2)}) collective-permute-start(s32[16,2]{0,1:T(2,128)} %param.17), channel_id=1, source_target_pairs={{1,0},{2,1},{3,2},{4,3},{5,4},{6,5},{7,6},{8,7},{9,8},{10,9},{11,1... | collective-permute-start | bytes 392 | tf_op jit(solution)/shard_map/ppermute | solution.py:14
  257.7 2.6 collective-permute-start.6
  259.0 5.9 %collective-permute-start.7 = (bf16[16,32,256]{2,1,0:T(8,128)(2,1)S(1)}, bf16[16,32,256]{2,1,0:T(8,128)(2,1)S(1)}, u32[]{:S(2)}, u32[]{:S(2)}) collective-permute-start(bf16[16,32,256]{2,1,0:T(8,128)(2,1)S(1)} %fusion.36), channel_id=1, source_target_pairs={{1,0},{2,1},{3,2},{4,3},{5,4},{6,5},{7,6},{8,7},{9,8},{10,9},{11,1... | collective-permute-start | bytes 786440 | tf_op jit(solution)/shard_map/ppermute | solution.py:14
where the time goes:
time: 347 us; the launch traced here: 345 us
  matrix products  124 us (36%)
  blocking collectives  84.8 us (24%)
  local copies, waits for them, and re-layouts  75.1 us (22%)
  other arithmetic  25.4 us (7%)
  starting transfers between devices  18.2 us (5%)
  waiting for transfers between devices  15.5 us (4%)
    psum x2, blocking collectives, orthonormal(): summed_gram = lax.psum(tile_gram, ('tiles', 'rep')) / total_points  84.8 us
    dot_general x9, matrix products, tapered(): jnp.einsum('hmi,hmj->hij', rows_one, rows_two, preferred_element_type=jnp...  79.1 us
    dot_general x18, matrix products, advance(): jnp.einsum('hkj,hij->hki', window_iter[at_here], block_here, preferred_el...  41.8 us
    dynamic_update_slice x18, local copies, waits for them, and re-layouts, form_blocks(): return (slot_at, lax.map(one_slot, slot_at))  38.9 us
    gather x9, local copies, waits for them, and re-layouts, one_slot(): window_rows[at_here]  19.2 us
    ppermute x8, starting transfers between devices, from_behind(): return lax.ppermute(shard, axis, pairs)  18.2 us
    ppermute x8, waiting for transfers between devices, from_behind(): return lax.ppermute(shard, axis, pairs)  15.5 us
    gather x18, local copies, waits for them, and re-layouts, advance(): window_iter[at_here]  10.1 us
  transfers between devices with their start and end apart: 8, of which 2 were waited for; matrix products, arithmetic and copies ran while one was open for 1% of the time, Pallas kernels for 0%

commit v1 on v0

v1 whole, which is shorter than its diff:
```python
import functools

import jax
import jax.numpy as jnp
from jax import lax
from jax.experimental import pallas as pl
from jax.experimental.pallas import tpu as pltpu
from jax.sharding import PartitionSpec as P

TILE_SIDE = 16
COLW = 8
ITERS = 2
AXES = ("tiles", "rep")
HIGH = lax.Precision.HIGHEST


def from_behind(shard, by):
    length = lax.axis_size(AXES)
    pairs = [(i, i + by) for i in range(length) if 0 <= i + by < length]
    return lax.ppermute(shard, AXES, pairs)


def gaspari(distance):
    scaled = distance / (0.5 * TILE_SIDE)
    clamped = jnp.maximum(scaled, 1.0)
    inner_part = (
        ((-0.25 * scaled + 0.5) * scaled + 0.625) * scaled - 5.0 / 3.0
    ) * scaled * scaled + 1.0
    outer_part = (
        ((((scaled / 12.0 - 0.5) * scaled + 0.625) * scaled + 5.0 / 3.0) * scaled - 5.0) * scaled
        + 4.0
        - 2.0 / (3.0 * clamped)
    )
    return jnp.where(scaled <= 1.0, inner_part, jnp.where(scaled <= 2.0, outer_part, 0.0))


def taper_kernel(scale, table_ref):
    step = pl.program_id(0)
    points = table_ref.shape[1]
    delta_x = step // 3 - 1
    delta_y = step % 3 - 1
    one = lax.broadcasted_iota(jnp.int32, (points, points), 0)
    two = lax.broadcasted_iota(jnp.int32, (points, points), 1)
    row = (delta_x * TILE_SIDE + one // TILE_SIDE - two // TILE_SIDE).astype(jnp.float32)
    col = (delta_y * TILE_SIDE + one % TILE_SIDE - two % TILE_SIDE).astype(jnp.float32)
    weight = gaspari(jnp.sqrt(row * row + col * col)) * scale
    table_ref[0] = jnp.where(step == 9, 0.0, weight)


def taper_table(points, scale):
    return pl.pallas_call(
        functools.partial(taper_kernel, scale),
        grid=(10,),
        out_shape=jax.ShapeDtypeStruct((10, points, points), jnp.float32),
        out_specs=pl.BlockSpec((1, points, points), lambda i: (i, 0, 0)),
        cost_estimate=pl.CostEstimate(
            flops=10 * 40 * points * points, bytes_accessed=40 * points * points, transcendentals=0
        ),
    )()


def gram_add(step, applied, gram_ref):
    part = lax.dot_general(
        applied, applied, (((1,), (1,)), ((), ())), precision=HIGH, preferred_element_type=jnp.float32
    )

    @pl.when(step == 0)
    def _():
        gram_ref[...] = part

    @pl.when(step != 0)
    def _():
        gram_ref[...] += part


def first_kernel(slot_ref, kind_ref, turned_ref, own_ref, iter_ref, table_ref, blocks_ref, applied_ref, gram_ref):
    step = pl.program_id(0)
    own = own_ref[0]
    total = None
    for s in range(slot_ref.shape[1]):
        at = slot_ref[step, s]
        product = jnp.dot(turned_ref[at], own, preferred_element_type=jnp.float32)
        block = (product * table_ref[kind_ref[step, s]]).astype(jnp.bfloat16)
        blocks_ref[0, s] = block
        part = jnp.dot(iter_ref[at], block, preferred_element_type=jnp.float32)
        total = part if total is None else total + part
    applied_ref[0] = total
    gram_add(step, total, gram_ref)


def later_kernel(slot_ref, iter_ref, blocks_ref, applied_ref, gram_ref):
    step = pl.program_id(0)
    total = None
    for s in range(slot_ref.shape[1]):
        part = jnp.dot(iter_ref[slot_ref[step, s]], blocks_ref[0, s], preferred_element_type=jnp.float32)
        total = part if total is None else total + part
    applied_ref[0] = total
    gram_add(step, total, gram_ref)


def norm_kernel(total_points, gram_ref, applied_ref, fresh_ref):
    rank = gram_ref.shape[0]
    rows = lax.broadcasted_iota(jnp.int32, (rank, rank), 0)
    cols = lax.broadcasted_iota(jnp.int32, (rank, rank), 1)
    left = gram_ref[...] / total_points
    work = jnp.concatenate([left, (rows == cols).astype(jnp.float32)], axis=1)
    down = lax.broadcasted_iota(jnp.int32, (rank, 1), 0)
    for j in range(rank):
        root = lax.sqrt(work[j : j + 1, j : j + 1])
        line = work[j : j + 1, :] / root
        factor = work[:, j : j + 1] / root
        work = jnp.where(down > j, work - factor * line, jnp.where(down == j, line, work))
    inverse = work[:, rank:]
    for a in range(applied_ref.shape[0]):
        fresh_ref[a] = jnp.dot(
            inverse, applied_ref[a], precision=HIGH, preferred_element_type=jnp.float32
        ).astype(fresh_ref.dtype)


def whole(shape):
    return pl.BlockSpec(shape, lambda i: (0,) * len(shape))


def per_tile(shape):
    return pl.BlockSpec((1,) + tuple(shape[1:]), lambda i: (i,) + (0,) * (len(shape) - 1))


def smem():
    return pl.BlockSpec(memory_space=pltpu.SMEM)


PARAMS = pltpu.CompilerParams(vmem_limit_bytes=40 * 1024 * 1024)


def window(own, edge):
    ahead = from_behind(own[:edge], -1)
    behind = from_behind(own[-edge:], 1)
    return behind, ahead


def local(members, initial, wet_counts, tile_coords, neighbours):
    tiles, count, points = members.shape
    rank = initial.shape[1]
    slots = neighbours.shape[1]
    edge = COLW + 2
    first_tile = lax.axis_index(AXES) * tiles
    total_points = float(tiles * lax.axis_size(AXES) * points)
    wet_mask = jnp.arange(points, dtype=jnp.int32)[None, :] < wet_counts[:, None]
    own_rows = jnp.where(wet_mask[:, None, :], members, jnp.zeros_like(members))
    join = lambda own, sides: jnp.concatenate([sides[0], own, sides[1]], 0)
    rows = join(own_rows, window(own_rows, edge))
    place = join(tile_coords, window(tile_coords, edge))
    current = join(initial, window(initial, edge))
    slot = jnp.clip(neighbours - (first_tile - edge), 0, tiles + 2 * edge - 1)
    delta = jnp.clip(place[slot] - tile_coords[:, None, :], -1, 1) + 1
    kind = jnp.where(neighbours >= 0, delta[..., 0] * 3 + delta[..., 1], 9)
    table = taper_table(points, 1.0 / (count - 1.0))
    turned = jnp.swapaxes(rows, 1, 2)
    applied_shape = jax.ShapeDtypeStruct((tiles, rank, points), jnp.float32)
    gram_shape = jax.ShapeDtypeStruct((rank, rank), jnp.float32)
    blocks_shape = jax.ShapeDtypeStruct((tiles, slots, points, points), jnp.bfloat16)
    blocks, applied, gram = pl.pallas_call(
        first_kernel,
        grid=(tiles,),
        in_specs=[
            smem(), smem(), whole(turned.shape), per_tile(own_rows.shape), whole(current.shape), whole(table.shape),
        ],
        out_specs=[per_tile(blocks_shape.shape), per_tile(applied_shape.shape), whole(gram_shape.shape)],
        out_shape=[blocks_shape, applied_shape, gram_shape],
        compiler_params=PARAMS,
    )(slot, kind, turned, own_rows, current, table)
    for sweep in range(ITERS):
        gram = lax.psum(gram, AXES)
        last = sweep == ITERS - 1
        fresh = pl.pallas_call(
            functools.partial(norm_kernel, total_points),
            out_shape=jax.ShapeDtypeStruct(
                applied_shape.shape, jnp.float32 if last else jnp.bfloat16
            ),
            compiler_params=PARAMS,
        )(gram, applied)
        if last:
            return fresh
        current = join(fresh, window(fresh, edge))
        applied, gram = pl.pallas_call(
            later_kernel,
            grid=(tiles,),
            in_specs=[smem(), whole(current.shape), per_tile(blocks.shape)],
            out_specs=[per_tile(applied_shape.shape), whole(gram_shape.shape)],
            out_shape=[applied_shape, gram_shape],
            compiler_params=PARAMS,
        )(slot, current, blocks)


def solution(mesh):
    spec = P(AXES, None, None)
    in_specs = (spec, spec, P(AXES), P(AXES, None), P(AXES, None))
    return jax.shard_map(local, mesh=mesh, in_specs=in_specs, out_specs=spec, check_vma=False)
```

time: 347 us -> 184 us (0.53)
  matrix products: 124 us -> 0 us
  local copies, waits for them, and re-layouts: 75.1 us -> 11.5 us
  Pallas kernels: 0 us -> 50.3 us
  other arithmetic: 25.4 us -> 4.37 us
  waiting for transfers between devices: 15.5 us -> 5.97 us
  blocking collectives: 84.8 us -> 92.9 us
    dot_general x31 -> x0, matrix products: 124 us -> none  [the longest x9 79.1 us: tapered(): jnp.einsum('hmi,hmj->hij', rows_one, rows_two, preferred_element_type=jnp...]
    pallas_call x0 -> x5, Pallas kernels: none -> 50.3 us  [the longest x1 20.6 us: local(): pl.pallas_call(first_kernel, grid=(tiles,), in_specs=[smem(), smem(), who...]
    dynamic_update_slice x18 -> x0, local copies, waits for them, and re-layouts: 38.9 us -> none  [form_blocks(): return (slot_at, lax.map(one_slot, slot_at))]
    gather x36 -> x3, local copies, waits for them, and re-layouts: 34.4 us -> 0.82 us  [local(): delta = jnp.clip(place[slot] - tile_coords[:, None, :], -1, 1) + 1]
    another operation x10 -> x0, other arithmetic: 13.4 us -> none  [the longest x6 7.19 us: orthonormal(): factor = jnp.linalg.cholesky(summed_gram)]
    ppermute x8, waiting for transfers between devices: 15.5 us -> 5.97 us  [from_behind(): return lax.ppermute(shard, AXES, pairs)]
    psum x2, blocking collectives: 84.8 us -> 92.9 us  [local(): gram = lax.psum(gram, AXES)]
    transpose x0 -> x1, local copies, waits for them, and re-layouts: none -> 3.99 us  [local(): turned = jnp.swapaxes(rows, 1, 2)]
  transfers between devices with their start and end apart: 8 -> 8, of which waited for: 2 -> 2; matrix products, arithmetic and copies ran while one was open for 1% -> 3% of each run, Pallas kernels for 0% -> 3%
where the time goes in v1:
time: 184 us
  blocking collectives  92.9 us (50%)
  Pallas kernels  50.3 us (27%)
  starting transfers between devices  18.2 us (10%)
  local copies, waits for them, and re-layouts  11.5 us (6%)
  waiting for transfers between devices  5.97 us (3%)
  other arithmetic  4.37 us (2%)
    psum x2, blocking collectives, local(): gram = lax.psum(gram, AXES)  92.9 us
    pallas_call x1, Pallas kernels, local(): pl.pallas_call(first_kernel, grid=(tiles,), in_specs=[smem(), smem(), who...  20.6 us
    ppermute x8, starting transfers between devices, from_behind(): return lax.ppermute(shard, AXES, pairs)  18.2 us
    pallas_call x1, Pallas kernels, local(): pl.pallas_call(later_kernel, grid=(tiles,), in_specs=[smem(), whole(curre...  15.4 us
    pallas_call x2, Pallas kernels, local(): pl.pallas_call(functools.partial(norm_kernel, total_points), out_shape=ja...  8.14 us
    pallas_call x1, Pallas kernels, taper_table(): pl.pallas_call(functools.partial(taper_kernel, scale), grid=(10,), out_sh...  6.07 us
    ppermute x8, waiting for transfers between devices, from_behind(): return lax.ppermute(shard, AXES, pairs)  5.97 us
    unnamed x16, local copies, waits for them, and re-layouts  4.58 us
  transfers between devices with their start and end apart: 8, of which 2 were waited for; matrix products, arithmetic and copies ran while one was open for 3% of the time, Pallas kernels for 3%

profile of v1, /device:TPU:0, one launch (start us, length us, event | category | flops | bytes accessed | tf_op | source)
XLA Modules:
  0.0 183.5 jit_solution(5561264645795154488)
XLA Ops:
  0.8 2.3 %collective-permute-start = (s32[10,2]{0,1:T(2,128)S(1)}, s32[10,2]{0,1:T(2,128)S(1)}, u32[]{:S(2)}, u32[]{:S(2)}) collective-permute-start(s32[10,2]{0,1:T(2,128)S(1)} %get-tuple-element.23), channel_id=1, source_target_pairs={{0,1},{1,2},{2,3},{3,4},{4,5},{5,6},{6,7},{7,8},{8,9},{9,10},{10,1... | collective-permute-start | bytes 248 | tf_op jit(solution)/shard_map/ppermute | solution.py:20
  3.2 1.3 collective-permute-start.1
  4.5 1.0 fusion.4
  5.5 5.1 %collective-permute-start.4 = (bf16[10,32,256]{2,1,0:T(8,128)(2,1)S(1)}, bf16[10,32,256]{2,1,0:T(8,128)(2,1)S(1)}, u32[]{:S(2)}, u32[]{:S(2)}) collective-permute-start(bf16[10,32,256]{2,1,0:T(8,128)(2,1)S(1)} %get-tuple-element.21), channel_id=1, source_target_pairs={{0,1},{1,2},{2,3},{3,4},{4,5},{5,6},{6,7},{7,8},{8,9},{9,10},{10,1... | collective-permute-start | bytes 491528 | tf_op jit(solution)/shard_map/ppermute | solution.py:20
  10.7 1.3 collective-permute-start.5
  12.7 1.2 broadcast_select_fusion.own_ref
  13.9 4.3 %collective-permute-start.2 = (bf16[10,80,256]{2,1,0:T(8,128)(2,1)S(1)}, bf16[10,80,256]{2,1,0:T(8,128)(2,1)S(1)}, u32[]{:S(2)}, u32[]{:S(2)}) collective-permute-start(bf16[10,80,256]{2,1,0:T(8,128)(2,1)S(1)} %get-tuple-element.17), channel_id=1, source_target_pairs={{0,1},{1,2},{2,3},{3,4},{4,5},{5,6},{6,7},{7,8},{8,9},{9,10},{10,1... | collective-permute-start | bytes 1228808 | tf_op jit(solution)/shard_map/ppermute | solution.py:20
  18.4 6.1 %shard_map.55.table_ref = f32[10,256,256]{2,1,0:T(8,128)} custom-call(), custom_call_target="tpu_custom_call" | custom-call | flops 26214400 | bytes 2621440 | tf_op jit(solution)/shard_map/pallas_call | solution.py:51
  24.4 1.3 collective-permute-start.3
  27.8 1.5 collective-permute-done.3
  29.3 1.3 maximum_bitcast_fusion
  30.6 4.0 %copy.18.turned_ref = bf16[36,256,80]{2,1,0:T(8,128)(2,1)} copy(bf16[36,256,80]{1,2,0:T(8,128)(2,1)} %maximum_bitcast_fusion) | data formatting | bytes 2949120 | tf_op jit(solution)/shard_map/transpose | solution.py:158
  34.6 1.7 copy-done.1
  36.3 1.1 copy-done.2
  37.3 20.6 %shard_map.56 = (bf16[16,9,256,256]{3,2,1,0:T(8,128)(2,1)}, f32[16,32,256]{2,1,0:T(8,128)S(1)}, f32[32,32]{1,0:T(8,128)S(1)}) custom-call(s32[16,9]{1,0:T(8,128)S(1)} %get-tuple-element.16.slot_ref, s32[16,9]{1,0:T(8,128)S(1)} %fusion.1.kind_ref, bf16[36,256,80]{2,1,0:T(8,128)(2,1)S(1)} %copy-done.1, bf16[16,80,256]{2,1,0:T(8,128)(2,1)S(1)} %broadcast_select_fusion.own_ref, ...), custom_call_target="tpu_custom_call" | custom-call | tf_op jit(solution)/shard_map/pallas_call | solution.py:162
  58.8 50.0 %psum.14.gram_ref = f32[32,32]{1,0:T(8,128)S(1)} all-reduce(f32[32,32]{1,0:T(8,128)S(1)} %get-tuple-element.10), channel_id=1, replica_groups=mesh['tiles'=16,'rep'=2] {'tiles','rep'}, use_global_device_ids=true, to_apply=%region_0.1 | all-reduce | flops 1024 | bytes 8192 | tf_op jit(solution)/shard_map/psum | solution.py:173
  108.8 1.0 copy-done.4
  109.8 3.7 %shard_map.57 = bf16[16,32,256]{2,1,0:T(8,128)(2,1)S(1)} custom-call(f32[32,32]{1,0:T(8,128)S(1)} %psum.14.gram_ref, f32[16,32,256]{2,1,0:T(8,128)S(1)} %copy-done.4), custom_call_target="tpu_custom_call" | custom-call | tf_op jit(solution)/shard_map/pallas_call | solution.py:175
  113.6 1.3 collective-permute-start.6
  114.9 1.3 collective-permute-start.7
  116.2 4.5 %collective-permute-done.7 = bf16[10,32,256]{2,1,0:T(8,128)(2,1)S(1)} collective-permute-done((bf16[10,32,256]{2,1,0:T(8,128)(2,1)S(1)}, bf16[10,32,256]{2,1,0:T(8,128)(2,1)S(1)}, u32[]{:S(2)}, u32[]{:S(2)}) %collective-permute-start.7) | collective-permute-done | bytes 163872 | tf_op jit(solution)/shard_map/ppermute | solution.py:20
  120.7 15.4 %shard_map.58 = (f32[16,32,256]{2,1,0:T(8,128)S(1)}, f32[32,32]{1,0:T(8,128)S(1)}) custom-call(s32[16,9]{1,0:T(8,128)S(1)} %get-tuple-element.16.slot_ref, bf16[36,32,256]{2,1,0:T(8,128)(2,1)S(1)} %pad_maximum_fusion.1.iter_ref, bf16[16,9,256,256]{3,2,1,0:T(8,128)(2,1)} %get-tuple-element.12.blocks_ref), custom_call_target="tpu_custom_call" | custom-call | tf_op jit(solution)/shard_map/pallas_call | solution.py:185
  136.2 42.9 %psum.15.gram_ref = f32[32,32]{1,0:T(8,128)S(1)} all-reduce(f32[32,32]{1,0:T(8,128)S(1)} %get-tuple-element.13), channel_id=1, replica_groups=mesh['tiles'=16,'rep'=2] {'tiles','rep'}, use_global_device_ids=true, to_apply=%region_1.2 | all-reduce | flops 1024 | bytes 8192 | tf_op jit(solution)/shard_map/psum | solution.py:173
  179.0 4.5 %shard_map.59 = f32[16,32,256]{2,1,0:T(8,128)} custom-call(f32[32,32]{1,0:T(8,128)S(1)} %psum.15.gram_ref, f32[16,32,256]{2,1,0:T(8,128)S(1)} %get-tuple-element.14.applied_ref), custom_call_target="tpu_custom_call" | custom-call | tf_op jit(solution)/shard_map/pallas_call | solution.py:175
  (35 shorter events, 4.6 us)
Async XLA Ops:
  0.8 23.6 %collective-permute-start = (s32[10,2]{0,1:T(2,128)S(1)}, s32[10,2]{0,1:T(2,128)S(1)}, u32[]{:S(2)}, u32[]{:S(2)}) collective-permute-start(s32[10,2]{0,1:T(2,128)S(1)} %get-tuple-element.23), channel_id=1, source_target_pairs={{0,1},{1,2},{2,3},{3,4},{4,5},{5,6},{6,7},{7,8},{8,9},{9,10},{10,1... | collective-permute-start | bytes 248 | tf_op jit(solution)/shard_map/ppermute | solution.py:20
  3.2 22.6 %collective-permute-start.1 = (s32[10,2]{0,1:T(2,128)S(1)}, s32[10,2]{0,1:T(2,128)S(1)}, u32[]{:S(2)}, u32[]{:S(2)}) collective-permute-start(s32[10,2]{0,1:T(2,128)S(1)} %get-tuple-element.24), channel_id=1, source_target_pairs={{1,0},{2,1},{3,2},{4,3},{5,4},{6,5},{7,6},{8,7},{9,8},{10,9},{11,1... | collective-permute-start | bytes 248 | tf_op jit(solution)/shard_map/ppermute | solution.py:20
  5.5 21.4 %collective-permute-start.4 = (bf16[10,32,256]{2,1,0:T(8,128)(2,1)S(1)}, bf16[10,32,256]{2,1,0:T(8,128)(2,1)S(1)}, u32[]{:S(2)}, u32[]{:S(2)}) collective-permute-start(bf16[10,32,256]{2,1,0:T(8,128)(2,1)S(1)} %get-tuple-element.21), channel_id=1, source_target_pairs={{0,1},{1,2},{2,3},{3,4},{4,5},{5,6},{6,7},{7,8},{8,9},{9,10},{10,1... | collective-permute-start | bytes 491528 | tf_op jit(solution)/shard_map/ppermute | solution.py:20
  10.7 16.2 %collective-permute-start.5 = (bf16[10,32,256]{2,1,0:T(8,128)(2,1)S(1)}, bf16[10,32,256]{2,1,0:T(8,128)(2,1)S(1)}, u32[]{:S(2)}, u32[]{:S(2)}) collective-permute-start(bf16[10,32,256]{2,1,0:T(8,128)(2,1)S(1)} %get-tuple-element.22), channel_id=1, source_target_pairs={{1,0},{2,1},{3,2},{4,3},{5,4},{6,5},{7,6},{8,7},{9,8},{10,9},{11,1... | collective-permute-start | bytes 491528 | tf_op jit(solution)/shard_map/ppermute | solution.py:20
  12.7 5.5 %copy-start.6 = (s32[16,9]{1,0:T(8,128)S(1)}, s32[16,9]{1,0:T(8,128)}, u32[]{:S(2)}) copy-start(s32[16,9]{1,0:T(8,128)} %param.9) | copy-start | bytes 1732
  13.9 11.8 %copy-start.7 = (s32[16,2]{0,1:T(2,128)S(1)}, s32[16,2]{0,1:T(2,128)}, u32[]{:S(2)}) copy-start(s32[16,2]{0,1:T(2,128)} %param.8) | copy-start | bytes 388
  13.9 13.9 %collective-permute-start.2 = (bf16[10,80,256]{2,1,0:T(8,128)(2,1)S(1)}, bf16[10,80,256]{2,1,0:T(8,128)(2,1)S(1)}, u32[]{:S(2)}, u32[]{:S(2)}) collective-permute-start(bf16[10,80,256]{2,1,0:T(8,128)(2,1)S(1)} %get-tuple-element.17), channel_id=1, source_target_pairs={{0,1},{1,2},{2,3},{3,4},{4,5},{5,6},{6,7},{7,8},{8,9},{9,10},{10,1... | collective-permute-start | bytes 1228808 | tf_op jit(solution)/shard_map/ppermute | solution.py:20
  18.4 8.5 %copy-start.5 = (bf16[16,32,256]{2,1,0:T(8,128)(2,1)S(1)}, bf16[16,32,256]{2,1,0:T(8,128)(2,1)}, u32[]{:S(2)}) copy-start(bf16[16,32,256]{2,1,0:T(8,128)(2,1)} %param.6) | copy-start | bytes 786436
  24.4 4.8 %collective-permute-start.3 = (bf16[10,80,256]{2,1,0:T(8,128)(2,1)S(1)}, bf16[10,80,256]{2,1,0:T(8,128)(2,1)S(1)}, u32[]{:S(2)}, u32[]{:S(2)}) collective-permute-start(bf16[10,80,256]{2,1,0:T(8,128)(2,1)S(1)} %get-tuple-element.18), channel_id=1, source_target_pairs={{1,0},{2,1},{3,2},{4,3},{5,4},{6,5},{7,6},{8,7},{9,8},{10,9},{11,1... | collective-permute-start | bytes 1228808 | tf_op jit(solution)/shard_map/ppermute | solution.py:20
  30.6 4.0 %copy-start = (f32[10,256,256]{2,1,0:T(8,128)S(1)}, f32[10,256,256]{2,1,0:T(8,128)}, u32[]{:S(2)}) copy-start(f32[10,256,256]{2,1,0:T(8,128)} %shard_map.55.table_ref) | copy-start | bytes 7864324
  34.6 1.7 copy-start.1
  36.3 1.1 copy-start.2
  58.0 0.8 copy-start.3
  108.8 1.0 copy-start.4
  113.6 2.6 %collective-permute-start.6 = (bf16[10,32,256]{2,1,0:T(8,128)(2,1)S(1)}, bf16[10,32,256]{2,1,0:T(8,128)(2,1)S(1)}, u32[]{:S(2)}, u32[]{:S(2)}) collective-permute-start(bf16[10,32,256]{2,1,0:T(8,128)(2,1)S(1)} %get-tuple-element.19), channel_id=1, source_target_pairs={{0,1},{1,2},{2,3},{3,4},{4,5},{5,6},{6,7},{7,8},{8,9},{9,10},{10,1... | collective-permute-start | bytes 491528 | tf_op jit(solution)/shard_map/ppermute | solution.py:20
  114.9 5.8 %collective-permute-start.7 = (bf16[10,32,256]{2,1,0:T(8,128)(2,1)S(1)}, bf16[10,32,256]{2,1,0:T(8,128)(2,1)S(1)}, u32[]{:S(2)}, u32[]{:S(2)}) collective-permute-start(bf16[10,32,256]{2,1,0:T(8,128)(2,1)S(1)} %get-tuple-element.20), channel_id=1, source_target_pairs={{1,0},{2,1},{3,2},{4,3},{5,4},{6,5},{7,6},{8,7},{9,8},{10,9},{11,1... | collective-permute-start | bytes 491528 | tf_op jit(solution)/shard_map/ppermute | solution.py:20

commit v2 on v1

--- a/solution.py
+++ b/solution.py
@@ -98,11 +98,53 @@
     gram_add(step, total, gram_ref)
 
 
-def norm_kernel(total_points, gram_ref, applied_ref, fresh_ref):
-    rank = gram_ref.shape[0]
+def device_at(index):
+    width = lax.axis_size(AXES[1])
+    return (index // width, index % width)
+
+
+def digit_groups(length):
+    groups = []
+    stride = 1
+    while stride < length:
+        size = next(s for s in range(min(8, length // stride), 1, -1) if (length // stride) % s == 0)
+        groups.append((stride, size))
+        stride *= size
+    return groups
+
+
+def exchange(me, source, inbox, send_sem, recv_sem, groups):
+    total = source[0]
+    for phase, (stride, size) in enumerate(groups):
+        digit = (me // stride) % size
+        if phase:
+            source[phase] = total
+        inbox[phase, digit] = total
+        copies = []
+        for hop in range(1, size):
+            other = me + ((digit + hop) % size - digit) * stride
+            copy = pltpu.make_async_remote_copy(
+                src_ref=source.at[phase],
+                dst_ref=inbox.at[phase, digit],
+                send_sem=send_sem.at[phase, hop],
+                recv_sem=recv_sem.at[phase, hop],
+                device_id=device_at(other),
+                device_id_type=pl.DeviceIdType.MESH,
+            )
+            copy.start()
+            copies.append(copy)
+        for copy in copies:
+            copy.wait()
+        total = inbox[phase, 0]
+        for at in range(1, size):
+            total = total + inbox[phase, at]
+    return total
+
+
+def inverse_factor(left):
+    rank = left.shape[0]
     rows = lax.broadcasted_iota(jnp.int32, (rank, rank), 0)
     cols = lax.broadcasted_iota(jnp.int32, (rank, rank), 1)
-    left = gram_ref[...] / total_points
     work = jnp.concatenate([left, (rows == cols).astype(jnp.float32)], axis=1)
     down = lax.broadcasted_iota(jnp.int32, (rank, 1), 0)
     for j in range(rank):
@@ -110,11 +152,104 @@
         line = work[j : j + 1, :] / root
         factor = work[:, j : j + 1] / root
         work = jnp.where(down > j, work - factor * line, jnp.where(down == j, line, work))
-    inverse = work[:, rank:]
-    for a in range(applied_ref.shape[0]):
-        fresh_ref[a] = jnp.dot(
+    return work[:, rank:]
+
+
+def norm_kernel(
+    total_points, groups, edge, gram_ref, applied_ref, fresh_ref,
+    source, inbox, halo, send_sem, recv_sem, halo_send, halo_recv,
+):
+    length = lax.axis_size(AXES)
+    me = lax.axis_index(AXES[0]) * lax.axis_size(AXES[1]) + lax.axis_index(AXES[1])
+    barrier = pltpu.get_barrier_semaphore()
+    mesh_ids = pl.DeviceIdType.MESH
+    greeted = 0
+    for stride, size in groups:
+        digit = (me // stride) % size
+        for hop in range(1, size):
+            other = me + ((digit + hop) % size - digit) * stride
+            pl.semaphore_signal(barrier, inc=1, device_id=device_at(other), device_id_type=mesh_ids)
+            greeted += 1
+    sides = ((me > 0, -1), (me < length - 1, 1)) if edge else ()
+    for there, by in sides:
+
+        @pl.when(there)
+        def _():
+            pl.semaphore_signal(barrier, inc=1, device_id=device_at(me + by), device_id_type=mesh_ids)
+
+    source[0] = gram_ref[...]
+    if edge:
+        greeted = greeted + jnp.minimum(me, 1) + jnp.minimum(length - 1 - me, 1)
+    pl.semaphore_wait(barrier, greeted)
+
+    inverse = inverse_factor(exchange(me, source, inbox, send_sem, recv_sem, groups) / total_points)
+    tiles = applied_ref.shape[0]
+
+    def put(a):
+        fresh_ref[a + edge] = jnp.dot(
             inverse, applied_ref[a], precision=HIGH, preferred_element_type=jnp.float32
         ).astype(fresh_ref.dtype)
+
+    if not edge:
+        for a in range(tiles):
+            put(a)
+        return
+
+    def shift(side):
+        first = edge if side == 0 else tiles
+        return pltpu.make_async_remote_copy(
+            src_ref=fresh_ref.at[pl.ds(first, edge)],
+            dst_ref=halo.at[1 - side],
+            send_sem=halo_send.at[side],
+            recv_sem=halo_recv.at[1 - side],
+            device_id=device_at(me + sides[side][1]),
+            device_id_type=mesh_ids,
+        )
+
+    for a in range(edge):
+        put(a)
+    pl.when(sides[0][0])(lambda: shift(0).start())
+    for a in range(edge, tiles):
+        put(a)
+    pl.when(sides[1][0])(lambda: shift(1).start())
+    for side in range(2):
+        landing = pl.ds(0 if side == 0 else edge + tiles, edge)
+
+        @pl.when(sides[side][0])
+        def _():
+            shift(side).wait_send()
+            shift(1 - side).wait_recv()
+            fresh_ref[landing] = halo[side]
+
+        @pl.when(jnp.logical_not(sides[side][0]))
+        def _():
+            fresh_ref[landing] = jnp.zeros(halo.shape[1:], halo.dtype)
+
+
+def normalise(gram, applied, total_points, edge, dtype, call_id):
+    tiles, rank, points = applied.shape
+    groups = digit_groups(lax.axis_size(AXES))
+    widest = max(size for _, size in groups)
+    sems = pltpu.SemaphoreType.DMA
+    vmem = pl.BlockSpec(memory_space=pltpu.VMEM)
+    return pl.pallas_call(
+        functools.partial(norm_kernel, total_points, groups, edge),
+        in_specs=[vmem, vmem],
+        out_specs=vmem,
+        out_shape=jax.ShapeDtypeStruct((tiles + 2 * edge, rank, points), dtype),
+        scratch_shapes=[
+            pltpu.VMEM((len(groups), rank, rank), jnp.float32),
+            pltpu.VMEM((len(groups), widest, rank, rank), jnp.float32),
+            pltpu.VMEM((2, max(edge, 1), rank, points), jnp.bfloat16),
+            sems((len(groups), widest)),
+            sems((len(groups), widest)),
+            sems((2,)),
+            sems((2,)),
+        ],
+        compiler_params=pltpu.CompilerParams(
+            collective_id=call_id, has_side_effects=True, vmem_limit_bytes=40 * 1024 * 1024
+        ),
+    )(gram, applied)
 
 
 def whole(shape):
@@ -151,7 +286,8 @@
     rows = join(own_rows, window(own_rows, edge))
     place = join(tile_coords, window(tile_coords, edge))
     current = join(initial, window(initial, edge))
-    slot = jnp.clip(neighbours - (first_tile - edge), 0, tiles + 2 * edge - 1)
+    slot = jnp.where(neighbours >= 0, neighbours - (first_tile - edge), edge)
+    slot = jnp.clip(slot, 0, tiles + 2 * edge - 1)
     delta = jnp.clip(place[slot] - tile_coords[:, None, :], -1, 1) + 1
     kind = jnp.where(neighbours >= 0, delta[..., 0] * 3 + delta[..., 1], 9)
     table = taper_table(points, 1.0 / (count - 1.0))
@@ -170,18 +306,9 @@
         compiler_params=PARAMS,
     )(slot, kind, turned, own_rows, current, table)
     for sweep in range(ITERS):
-        gram = lax.psum(gram, AXES)
-        last = sweep == ITERS - 1
-        fresh = pl.pallas_call(
-            functools.partial(norm_kernel, total_points),
-            out_shape=jax.ShapeDtypeStruct(
-                applied_shape.shape, jnp.float32 if last else jnp.bfloat16
-            ),
-            compiler_params=PARAMS,
-        )(gram, applied)
-        if last:
-            return fresh
-        current = join(fresh, window(fresh, edge))
+        if sweep == ITERS - 1:
+            return normalise(gram, applied, total_points, 0, jnp.float32, sweep)
+        current = normalise(gram, applied, total_points, edge, jnp.bfloat16, sweep)
         applied, gram = pl.pallas_call(
             later_kernel,
             grid=(tiles,),

time: 184 us -> 118 us (0.64)
  blocking collectives: 92.9 us -> 0 us
  Pallas kernels: 50.3 us -> 85.3 us
  waiting for transfers between devices: 5.97 us -> 1.49 us
  starting transfers between devices: 18.2 us -> 15.6 us
    psum x2 -> x0, blocking collectives: 92.9 us -> none  [local(): gram = lax.psum(gram, AXES)]
    pallas_call x2, Pallas kernels: 8.14 us -> 43.2 us  [normalise(): pl.pallas_call(functools.partial(norm_kernel, total_points, groups, edge)...]
    ppermute x8 -> x6, waiting for transfers between devices: 5.97 us -> 1.49 us  [from_behind(): return lax.ppermute(shard, AXES, pairs)]
    ppermute x8 -> x6, starting transfers between devices: 18.2 us -> 15.6 us  [from_behind(): return lax.ppermute(shard, AXES, pairs)]
    unnamed x16 -> x13, local copies, waits for them, and re-layouts: 4.58 us -> 3.54 us
  transfers between devices with their start and end apart: 8 -> 6, of which waited for: 2 -> 1; matrix products, arithmetic and copies ran while one was open for 3% -> 4% of each run, Pallas kernels for 3% -> 5%
where the time goes in v2:
time: 118 us; the launch traced here: 117 us
  Pallas kernels  85.3 us (72%)
  starting transfers between devices  15.6 us (13%)
  local copies, waits for them, and re-layouts  10.4 us (9%)
  other arithmetic  4.3 us (4%)
  waiting for transfers between devices  1.49 us (1%)
    pallas_call x2, Pallas kernels, normalise(): pl.pallas_call(functools.partial(norm_kernel, total_points, groups, edge)...  43.2 us
    pallas_call x1, Pallas kernels, local(): pl.pallas_call(first_kernel, grid=(tiles,), in_specs=[smem(), smem(), who...  20.6 us
    ppermute x6, starting transfers between devices, from_behind(): return lax.ppermute(shard, AXES, pairs)  15.6 us
    pallas_call x1, Pallas kernels, local(): pl.pallas_call(later_kernel, grid=(tiles,), in_specs=[smem(), whole(curre...  15.4 us
    pallas_call x1, Pallas kernels, taper_table(): pl.pallas_call(functools.partial(taper_kernel, scale), grid=(10,), out_sh...  6.07 us
    transpose x1, local copies, waits for them, and re-layouts, local(): turned = jnp.swapaxes(rows, 1, 2)  3.99 us
    unnamed x13, local copies, waits for them, and re-layouts  3.54 us
  transfers between devices with their start and end apart: 6, of which 1 were waited for; matrix products, arithmetic and copies ran while one was open for 4% of the time, Pallas kernels for 5%

profile of v2, /device:TPU:0, one launch (start us, length us, event | category | flops | bytes accessed | tf_op | source)
XLA Modules:
  0.0 117.3 jit_solution(17810850564513223107)
XLA Ops:
  0.0 0.8 fusion.4
  0.8 2.3 %collective-permute-start = (s32[10,2]{0,1:T(2,128)S(1)}, s32[10,2]{0,1:T(2,128)S(1)}, u32[]{:S(2)}, u32[]{:S(2)}) collective-permute-start(s32[10,2]{0,1:T(2,128)S(1)} %get-tuple-element.21), channel_id=1, source_target_pairs={{0,1},{1,2},{2,3},{3,4},{4,5},{5,6},{6,7},{7,8},{8,9},{9,10},{10,1... | collective-permute-start | bytes 248 | tf_op jit(solution)/shard_map/ppermute | solution.py:20
  3.2 1.3 %collective-permute-start.1 = (s32[10,2]{0,1:T(2,128)S(1)}, s32[10,2]{0,1:T(2,128)S(1)}, u32[]{:S(2)}, u32[]{:S(2)}) collective-permute-start(s32[10,2]{0,1:T(2,128)S(1)} %get-tuple-element.22), channel_id=1, source_target_pairs={{1,0},{2,1},{3,2},{4,3},{5,4},{6,5},{7,6},{8,7},{9,8},{10,9},{11,1... | collective-permute-start | bytes 248 | tf_op jit(solution)/shard_map/ppermute | solution.py:20
  4.5 1.0 fusion.3
  5.5 5.1 %collective-permute-start.4 = (bf16[10,32,256]{2,1,0:T(8,128)(2,1)S(1)}, bf16[10,32,256]{2,1,0:T(8,128)(2,1)S(1)}, u32[]{:S(2)}, u32[]{:S(2)}) collective-permute-start(bf16[10,32,256]{2,1,0:T(8,128)(2,1)S(1)} %get-tuple-element.19), channel_id=1, source_target_pairs={{0,1},{1,2},{2,3},{3,4},{4,5},{5,6},{6,7},{7,8},{8,9},{9,10},{10,1... | collective-permute-start | bytes 491528 | tf_op jit(solution)/shard_map/ppermute | solution.py:20
  10.7 1.3 %collective-permute-start.5 = (bf16[10,32,256]{2,1,0:T(8,128)(2,1)S(1)}, bf16[10,32,256]{2,1,0:T(8,128)(2,1)S(1)}, u32[]{:S(2)}, u32[]{:S(2)}) collective-permute-start(bf16[10,32,256]{2,1,0:T(8,128)(2,1)S(1)} %get-tuple-element.20), channel_id=1, source_target_pairs={{1,0},{2,1},{3,2},{4,3},{5,4},{6,5},{7,6},{8,7},{9,8},{10,9},{11,1... | collective-permute-start | bytes 491528 | tf_op jit(solution)/shard_map/ppermute | solution.py:20
  12.0 0.7 iota_compare_fusion
  12.7 1.2 broadcast_select_fusion.own_ref
  13.9 4.3 %collective-permute-start.2 = (bf16[10,80,256]{2,1,0:T(8,128)(2,1)S(1)}, bf16[10,80,256]{2,1,0:T(8,128)(2,1)S(1)}, u32[]{:S(2)}, u32[]{:S(2)}) collective-permute-start(bf16[10,80,256]{2,1,0:T(8,128)(2,1)S(1)} %get-tuple-element.17), channel_id=1, source_target_pairs={{0,1},{1,2},{2,3},{3,4},{4,5},{5,6},{6,7},{7,8},{8,9},{9,10},{10,1... | collective-permute-start | bytes 1228808 | tf_op jit(solution)/shard_map/ppermute | solution.py:20
  18.4 6.1 %shard_map.55.table_ref = f32[10,256,256]{2,1,0:T(8,128)} custom-call(), custom_call_target="tpu_custom_call" | custom-call | flops 26214400 | bytes 2621440 | tf_op jit(solution)/shard_map/pallas_call | solution.py:51
  24.4 1.3 %collective-permute-start.3 = (bf16[10,80,256]{2,1,0:T(8,128)(2,1)S(1)}, bf16[10,80,256]{2,1,0:T(8,128)(2,1)S(1)}, u32[]{:S(2)}, u32[]{:S(2)}) collective-permute-start(bf16[10,80,256]{2,1,0:T(8,128)(2,1)S(1)} %get-tuple-element.18), channel_id=1, source_target_pairs={{1,0},{2,1},{3,2},{4,3},{5,4},{6,5},{7,6},{8,7},{9,8},{10,9},{11,1... | collective-permute-start | bytes 1228808 | tf_op jit(solution)/shard_map/ppermute | solution.py:20
  25.8 0.1 copy.16
  25.9 0.7 gather_fusion
  26.9 0.9 pad_maximum_fusion.iter_ref
  27.8 1.5 %collective-permute-done.3 = bf16[10,80,256]{2,1,0:T(8,128)(2,1)S(1)} collective-permute-done((bf16[10,80,256]{2,1,0:T(8,128)(2,1)S(1)}, bf16[10,80,256]{2,1,0:T(8,128)(2,1)S(1)}, u32[]{:S(2)}, u32[]{:S(2)}) %collective-permute-start.3) | collective-permute-done | bytes 409632 | tf_op jit(solution)/shard_map/ppermute | solution.py:20
  29.3 1.3 %maximum_bitcast_fusion = bf16[36,256,80]{1,2,0:T(8,128)(2,1)} fusion(bf16[10,80,256]{2,1,0:T(8,128)(2,1)S(1)} %collective-permute-done.3, bf16[16,80,256]{2,1,0:T(8,128)(2,1)S(1)} %broadcast_select_fusion.own_ref, bf16[10,80,256]{2,1,0:T(8,128)(2,1)S(1)} %collective-permute-done.2), kind=kLoop, calls=%fused_computation.1 | loop fusion | flops 1474560 | bytes 2949120 | tf_op jit(solution)/shard_map/transpose | solution.py:294
  30.6 4.0 %copy.18.turned_ref = bf16[36,256,80]{2,1,0:T(8,128)(2,1)} copy(bf16[36,256,80]{1,2,0:T(8,128)(2,1)} %maximum_bitcast_fusion) | data formatting | bytes 2949120 | tf_op jit(solution)/shard_map/transpose | solution.py:294
  34.6 1.7 %copy-done.1 = bf16[36,256,80]{2,1,0:T(8,128)(2,1)S(1)} copy-done((bf16[36,256,80]{2,1,0:T(8,128)(2,1)S(1)}, bf16[36,256,80]{2,1,0:T(8,128)(2,1)}, u32[]{:S(2)}) %copy-start.1) | copy-done | bytes 1474584
  36.3 1.1 copy-done.2
  37.3 20.6 %shard_map.56 = (bf16[16,9,256,256]{3,2,1,0:T(8,128)(2,1)}, f32[16,32,256]{2,1,0:T(8,128)S(1)}, f32[32,32]{1,0:T(8,128)S(1)}) custom-call(s32[16,9]{1,0:T(8,128)S(1)} %get-tuple-element.16.slot_ref, s32[16,9]{1,0:T(8,128)S(1)} %fusion.1.kind_ref, bf16[36,256,80]{2,1,0:T(8,128)(2,1)S(1)} %copy-done.1, bf16[16,80,256]{2,1,0:T(8,128)(2,1)S(1)} %broadcast_select_fusion.own_ref, ...), custom_call_target="tpu_custom_call" | custom-call | tf_op jit(solution)/shard_map/pallas_call | solution.py:298
  58.0 26.2 %shard_map.57.iter_ref = bf16[36,32,256]{2,1,0:T(8,128)(2,1)S(1)} custom-call(f32[32,32]{1,0:T(8,128)S(1)} %get-tuple-element.10.gram_ref, f32[16,32,256]{2,1,0:T(8,128)S(1)} %get-tuple-element.11.applied_ref), custom_call_target="tpu_custom_call" | custom-call | tf_op jit(solution)/shard_map/pallas_call | solution.py:235
  84.2 15.4 %shard_map.58 = (f32[16,32,256]{2,1,0:T(8,128)S(1)}, f32[32,32]{1,0:T(8,128)S(1)}) custom-call(s32[16,9]{1,0:T(8,128)S(1)} %get-tuple-element.16.slot_ref, bf16[36,32,256]{2,1,0:T(8,128)(2,1)S(1)} %shard_map.57.iter_ref, bf16[16,9,256,256]{3,2,1,0:T(8,128)(2,1)} %get-tuple-element.12.blocks_ref), custom_call_target="tpu_custom_call" | custom-call | tf_op jit(solution)/shard_map/pallas_call | solution.py:312
  99.6 16.9 %shard_map.59 = f32[16,32,256]{2,1,0:T(8,128)S(1)} custom-call(f32[32,32]{1,0:T(8,128)S(1)} %get-tuple-element.13.gram_ref, f32[16,32,256]{2,1,0:T(8,128)S(1)} %get-tuple-element.14.applied_ref), custom_call_target="tpu_custom_call" | custom-call | tf_op jit(solution)/shard_map/pallas_call | solution.py:235
  116.6 0.8 copy.20
  (24 shorter events, 0.5 us)
Async XLA Ops:
  0.8 23.6 %collective-permute-start = (s32[10,2]{0,1:T(2,128)S(1)}, s32[10,2]{0,1:T(2,128)S(1)}, u32[]{:S(2)}, u32[]{:S(2)}) collective-permute-start(s32[10,2]{0,1:T(2,128)S(1)} %get-tuple-element.21), channel_id=1, source_target_pairs={{0,1},{1,2},{2,3},{3,4},{4,5},{5,6},{6,7},{7,8},{8,9},{9,10},{10,1... | collective-permute-start | bytes 248 | tf_op jit(solution)/shard_map/ppermute | solution.py:20
  3.2 22.6 %collective-permute-start.1 = (s32[10,2]{0,1:T(2,128)S(1)}, s32[10,2]{0,1:T(2,128)S(1)}, u32[]{:S(2)}, u32[]{:S(2)}) collective-permute-start(s32[10,2]{0,1:T(2,128)S(1)} %get-tuple-element.22), channel_id=1, source_target_pairs={{1,0},{2,1},{3,2},{4,3},{5,4},{6,5},{7,6},{8,7},{9,8},{10,9},{11,1... | collective-permute-start | bytes 248 | tf_op jit(solution)/shard_map/ppermute | solution.py:20
  5.5 21.4 %collective-permute-start.4 = (bf16[10,32,256]{2,1,0:T(8,128)(2,1)S(1)}, bf16[10,32,256]{2,1,0:T(8,128)(2,1)S(1)}, u32[]{:S(2)}, u32[]{:S(2)}) collective-permute-start(bf16[10,32,256]{2,1,0:T(8,128)(2,1)S(1)} %get-tuple-element.19), channel_id=1, source_target_pairs={{0,1},{1,2},{2,3},{3,4},{4,5},{5,6},{6,7},{7,8},{8,9},{9,10},{10,1... | collective-permute-start | bytes 491528 | tf_op jit(solution)/shard_map/ppermute | solution.py:20
  10.7 16.2 %collective-permute-start.5 = (bf16[10,32,256]{2,1,0:T(8,128)(2,1)S(1)}, bf16[10,32,256]{2,1,0:T(8,128)(2,1)S(1)}, u32[]{:S(2)}, u32[]{:S(2)}) collective-permute-start(bf16[10,32,256]{2,1,0:T(8,128)(2,1)S(1)} %get-tuple-element.20), channel_id=1, source_target_pairs={{1,0},{2,1},{3,2},{4,3},{5,4},{6,5},{7,6},{8,7},{9,8},{10,9},{11,1... | collective-permute-start | bytes 491528 | tf_op jit(solution)/shard_map/ppermute | solution.py:20
  12.7 5.5 %copy-start.4 = (s32[16,9]{1,0:T(8,128)S(1)}, s32[16,9]{1,0:T(8,128)}, u32[]{:S(2)}) copy-start(s32[16,9]{1,0:T(8,128)} %param.9) | copy-start | bytes 1732
  13.9 11.8 %copy-start.5 = (s32[16,2]{0,1:T(2,128)S(1)}, s32[16,2]{0,1:T(2,128)}, u32[]{:S(2)}) copy-start(s32[16,2]{0,1:T(2,128)} %param.8) | copy-start | bytes 388
  13.9 13.9 %collective-permute-start.2 = (bf16[10,80,256]{2,1,0:T(8,128)(2,1)S(1)}, bf16[10,80,256]{2,1,0:T(8,128)(2,1)S(1)}, u32[]{:S(2)}, u32[]{:S(2)}) collective-permute-start(bf16[10,80,256]{2,1,0:T(8,128)(2,1)S(1)} %get-tuple-element.17), channel_id=1, source_target_pairs={{0,1},{1,2},{2,3},{3,4},{4,5},{5,6},{6,7},{7,8},{8,9},{9,10},{10,1... | collective-permute-start | bytes 1228808 | tf_op jit(solution)/shard_map/ppermute | solution.py:20
  18.4 8.5 %copy-start.3 = (bf16[16,32,256]{2,1,0:T(8,128)(2,1)S(1)}, bf16[16,32,256]{2,1,0:T(8,128)(2,1)}, u32[]{:S(2)}) copy-start(bf16[16,32,256]{2,1,0:T(8,128)(2,1)} %param.6) | copy-start | bytes 786436
  24.4 4.8 %collective-permute-start.3 = (bf16[10,80,256]{2,1,0:T(8,128)(2,1)S(1)}, bf16[10,80,256]{2,1,0:T(8,128)(2,1)S(1)}, u32[]{:S(2)}, u32[]{:S(2)}) collective-permute-start(bf16[10,80,256]{2,1,0:T(8,128)(2,1)S(1)} %get-tuple-element.18), channel_id=1, source_target_pairs={{1,0},{2,1},{3,2},{4,3},{5,4},{6,5},{7,6},{8,7},{9,8},{10,9},{11,1... | collective-permute-start | bytes 1228808 | tf_op jit(solution)/shard_map/ppermute | solution.py:20
  30.6 4.0 %copy-start = (f32[10,256,256]{2,1,0:T(8,128)S(1)}, f32[10,256,256]{2,1,0:T(8,128)}, u32[]{:S(2)}) copy-start(f32[10,256,256]{2,1,0:T(8,128)} %shard_map.55.table_ref) | copy-start | bytes 7864324
  34.6 1.7 %copy-start.1 = (bf16[36,256,80]{2,1,0:T(8,128)(2,1)S(1)}, bf16[36,256,80]{2,1,0:T(8,128)(2,1)}, u32[]{:S(2)}) copy-start(bf16[36,256,80]{2,1,0:T(8,128)(2,1)} %copy.18.turned_ref) | copy-start | bytes 4423684
  36.3 1.1 copy-start.2

commit v3 on v2

--- a/solution.py
+++ b/solution.py
@@ -12,12 +12,6 @@
 ITERS = 2
 AXES = ("tiles", "rep")
 HIGH = lax.Precision.HIGHEST
-
-
-def from_behind(shard, by):
-    length = lax.axis_size(AXES)
-    pairs = [(i, i + by) for i in range(length) if 0 <= i + by < length]
-    return lax.ppermute(shard, AXES, pairs)
 
 
 def gaspari(distance):
@@ -34,29 +28,121 @@
     return jnp.where(scaled <= 1.0, inner_part, jnp.where(scaled <= 2.0, outer_part, 0.0))
 
 
-def taper_kernel(scale, table_ref):
-    step = pl.program_id(0)
-    points = table_ref.shape[1]
+def taper_at(step, points, scale):
     delta_x = step // 3 - 1
     delta_y = step % 3 - 1
     one = lax.broadcasted_iota(jnp.int32, (points, points), 0)
     two = lax.broadcasted_iota(jnp.int32, (points, points), 1)
     row = (delta_x * TILE_SIDE + one // TILE_SIDE - two // TILE_SIDE).astype(jnp.float32)
     col = (delta_y * TILE_SIDE + one % TILE_SIDE - two % TILE_SIDE).astype(jnp.float32)
-    weight = gaspari(jnp.sqrt(row * row + col * col)) * scale
-    table_ref[0] = jnp.where(step == 9, 0.0, weight)
-
-
-def taper_table(points, scale):
+    return gaspari(jnp.sqrt(row * row + col * col)) * scale
+
+
+def open_kernel(
+    edge, scale, wet_ref, members_ref, initial_ref, place_ref,
+    own_ref, turned_ref, iter_ref, places_ref, table_ref,
+    halo_rows, halo_iter, halo_place, send_sem, recv_sem,
+):
+    length = lax.axis_size(AXES)
+    me = lax.axis_index(AXES[0]) * lax.axis_size(AXES[1]) + lax.axis_index(AXES[1])
+    mesh_ids = pl.DeviceIdType.MESH
+    barrier = pltpu.get_barrier_semaphore()
+    sides = ((me > 0, -1), (me < length - 1, 1))
+    for there, by in sides:
+
+        @pl.when(there)
+        def _():
+            pl.semaphore_signal(barrier, inc=1, device_id=device_at(me + by), device_id_type=mesh_ids)
+
+    tiles, count, points = members_ref.shape
+    point = lax.broadcasted_iota(jnp.int32, (count, points), 1)
+    for a in range(tiles):
+        rows = members_ref[a].astype(jnp.float32)
+        own_ref[a] = jnp.where(point < wet_ref[a], rows, 0.0).astype(jnp.bfloat16)
+    pl.semaphore_wait(barrier, jnp.minimum(me, 1) + jnp.minimum(length - 1 - me, 1))
+
+    pairs = ((own_ref, halo_rows), (initial_ref, halo_iter), (place_ref, halo_place))
+
+    def shift(side, k):
+        first = 0 if side == 0 else tiles - edge
+        return pltpu.make_async_remote_copy(
+            src_ref=pairs[k][0].at[pl.ds(first, edge)],
+            dst_ref=pairs[k][1].at[1 - side],
+            send_sem=send_sem.at[side, k],
+            recv_sem=recv_sem.at[1 - side, k],
+            device_id=device_at(me + sides[side][1]),
+            device_id_type=mesh_ids,
+        )
+
+    for side in range(2):
+
+        @pl.when(sides[side][0])
+        def _():
+            for k in range(3):
+                shift(side, k).start()
+
+    def turn(rows):
+        return rows.astype(jnp.float32).T.astype(jnp.bfloat16)
+
+    for a in range(tiles):
+        turned_ref[edge + a] = turn(own_ref[a])
+    iter_ref[pl.ds(edge, tiles)] = initial_ref[...]
+    places_ref[pl.ds(edge, tiles)] = place_ref[...]
+
+    @pl.loop(0, 9)
+    def _(step):
+        table_ref[step] = taper_at(step, points, scale)
+
+    table_ref[9] = jnp.zeros((points, points), jnp.float32)
+
+    for side in range(2):
+        first = 0 if side == 0 else edge + tiles
+
+        @pl.when(sides[side][0])
+        def _():
+            for k in range(3):
+                shift(side, k).wait_send()
+                shift(1 - side, k).wait_recv()
+            for a in range(edge):
+                turned_ref[first + a] = turn(halo_rows[side, a])
+            iter_ref[pl.ds(first, edge)] = halo_iter[side]
+            places_ref[pl.ds(first, edge)] = halo_place[side]
+
+        @pl.when(jnp.logical_not(sides[side][0]))
+        def _():
+            turned_ref[pl.ds(first, edge)] = jnp.zeros((edge, points, count), jnp.bfloat16)
+            iter_ref[pl.ds(first, edge)] = jnp.zeros(halo_iter.shape[1:], jnp.bfloat16)
+            places_ref[pl.ds(first, edge)] = jnp.zeros(halo_place.shape[1:], jnp.int32)
+
+
+def opening(members, initial, wet_counts, tile_coords, edge, call_id):
+    tiles, count, points = members.shape
+    rank = initial.shape[1]
+    span = tiles + 2 * edge
+    place = jnp.pad(tile_coords, ((0, 0), (0, 126)))[:, None, :]
+    vmem = pl.BlockSpec(memory_space=pltpu.VMEM)
     return pl.pallas_call(
-        functools.partial(taper_kernel, scale),
-        grid=(10,),
-        out_shape=jax.ShapeDtypeStruct((10, points, points), jnp.float32),
-        out_specs=pl.BlockSpec((1, points, points), lambda i: (i, 0, 0)),
-        cost_estimate=pl.CostEstimate(
-            flops=10 * 40 * points * points, bytes_accessed=40 * points * points, transcendentals=0
+        functools.partial(open_kernel, edge, 1.0 / (count - 1.0)),
+        in_specs=[smem(), vmem, vmem, vmem],
+        out_specs=[vmem] * 5,
+        out_shape=[
+            jax.ShapeDtypeStruct(members.shape, jnp.bfloat16),
+            jax.ShapeDtypeStruct((span, points, count), jnp.bfloat16),
+            jax.ShapeDtypeStruct((span, rank, points), jnp.bfloat16),
+            jax.ShapeDtypeStruct((span, 1, 128), jnp.int32),
+            jax.ShapeDtypeStruct((10, points, points), jnp.float32),
+        ],
+        scratch_shapes=[
+            pltpu.VMEM((2, edge, count, points), jnp.bfloat16),
+            pltpu.VMEM((2, edge, rank, points), jnp.bfloat16),
+            pltpu.VMEM((2, edge, 1, 128), jnp.int32),
+            pltpu.SemaphoreType.DMA((2, 3)),
+            pltpu.SemaphoreType.DMA((2, 3)),
+        ],
+        compiler_params=pltpu.CompilerParams(
+            collective_id=call_id, has_side_effects=True, vmem_limit_bytes=40 * 1024 * 1024
         ),
-    )()
+    )(wet_counts, members, initial, place)
 
 
 def gram_add(step, applied, gram_ref):
@@ -267,12 +353,6 @@
 PARAMS = pltpu.CompilerParams(vmem_limit_bytes=40 * 1024 * 1024)
 
 
-def window(own, edge):
-    ahead = from_behind(own[:edge], -1)
-    behind = from_behind(own[-edge:], 1)
-    return behind, ahead
-
-
 def local(members, initial, wet_counts, tile_coords, neighbours):
     tiles, count, points = members.shape
     rank = initial.shape[1]
@@ -280,18 +360,14 @@
     edge = COLW + 2
     first_tile = lax.axis_index(AXES) * tiles
     total_points = float(tiles * lax.axis_size(AXES) * points)
-    wet_mask = jnp.arange(points, dtype=jnp.int32)[None, :] < wet_counts[:, None]
-    own_rows = jnp.where(wet_mask[:, None, :], members, jnp.zeros_like(members))
-    join = lambda own, sides: jnp.concatenate([sides[0], own, sides[1]], 0)
-    rows = join(own_rows, window(own_rows, edge))
-    place = join(tile_coords, window(tile_coords, edge))
-    current = join(initial, window(initial, edge))
+    own_rows, turned, current, place, table = opening(
+        members, initial, wet_counts, tile_coords, edge, ITERS
+    )
+    place = place[:, 0, :2]
     slot = jnp.where(neighbours >= 0, neighbours - (first_tile - edge), edge)
     slot = jnp.clip(slot, 0, tiles + 2 * edge - 1)
     delta = jnp.clip(place[slot] - tile_coords[:, None, :], -1, 1) + 1
     kind = jnp.where(neighbours >= 0, delta[..., 0] * 3 + delta[..., 1], 9)
-    table = taper_table(points, 1.0 / (count - 1.0))
-    turned = jnp.swapaxes(rows, 1, 2)
     applied_shape = jax.ShapeDtypeStruct((tiles, rank, points), jnp.float32)
     gram_shape = jax.ShapeDtypeStruct((rank, rank), jnp.float32)
     blocks_shape = jax.ShapeDtypeStruct((tiles, slots, points, points), jnp.bfloat16)

time: 118 us -> 100 us (0.85)
  starting transfers between devices: 15.6 us -> 0 us
  other arithmetic: 4.3 us -> 2.18 us
  waiting for transfers between devices: 1.49 us -> 0 us
  Pallas kernels: 85.3 us -> 86.7 us
    ppermute x6 -> x0, starting transfers between devices: 15.6 us -> none  [from_behind(): return lax.ppermute(shard, AXES, pairs)]
    unnamed x13 -> x16, local copies, waits for them, and re-layouts: 3.54 us -> 9.21 us
    transpose x1 -> x0, local copies, waits for them, and re-layouts: 3.99 us -> none  [local(): turned = jnp.swapaxes(rows, 1, 2)]
    pallas_call x2, Pallas kernels: 43.2 us -> 45.1 us  [normalise(): pl.pallas_call(functools.partial(norm_kernel, total_points, groups, edge)...]
    slice x3 -> x1, local copies, waits for them, and re-layouts: 1.9 us -> 0.08 us  [local(): place = place[:, 0, :2]]
    ppermute x6 -> x0, waiting for transfers between devices: 1.49 us -> none  [from_behind(): return lax.ppermute(shard, AXES, pairs)]
    transpose x1 -> x0, other arithmetic: 1.33 us -> none  [local(): turned = jnp.swapaxes(rows, 1, 2)]
  transfers between devices with their start and end apart: 6 -> 0, of which waited for: 1 -> 0; matrix products, arithmetic and copies ran while one was open for 4% -> 0% of each run, Pallas kernels for 5% -> 0%
where the time goes in v3:
time: 100 us; the launch traced here: 99.3 us
  Pallas kernels  86.7 us (87%)
  local copies, waits for them, and re-layouts  10.3 us (10%)
  other arithmetic  2.18 us (2%)
    pallas_call x2, Pallas kernels, normalise(): pl.pallas_call(functools.partial(norm_kernel, total_points, groups, edge)...  45.1 us
    pallas_call x1, Pallas kernels, local(): pl.pallas_call(first_kernel, grid=(tiles,), in_specs=[smem(), smem(), who...  20.6 us
    pallas_call x1, Pallas kernels, local(): pl.pallas_call(later_kernel, grid=(tiles,), in_specs=[smem(), whole(curre...  15.4 us
    unnamed x16, local copies, waits for them, and re-layouts  9.21 us
    pallas_call x1, Pallas kernels, opening(): pl.pallas_call(functools.partial(open_kernel, edge, 1.0 / (count - 1.0)),...  5.55 us

profile of v3, /device:TPU:0, one launch (start us, length us, event | category | flops | bytes accessed | tf_op | source)
XLA Modules:
  0.0 99.3 jit_solution(15307569809150923737)
XLA Ops:
  0.0 0.8 copy.10
  0.8 0.7 compare_select_fusion
  1.5 0.1 reshape.6
  1.6 0.0 copy-start.2
  1.6 1.1 %copy-done.2 = bf16[16,80,256]{2,1,0:T(8,128)(2,1)S(1)} copy-done((bf16[16,80,256]{2,1,0:T(8,128)(2,1)S(1)}, bf16[16,80,256]{2,1,0:T(8,128)(2,1)}, u32[]{:S(2)}) %copy-start.2) | copy-done | bytes 655384
  2.7 0.9 copy-done.5
  3.6 0.7 copy-done.6
  4.3 5.6 %shard_map.55 = (bf16[16,80,256]{2,1,0:T(8,128)(2,1)S(1)}, bf16[36,256,80]{2,1,0:T(8,128)(2,1)S(1)}, bf16[36,32,256]{2,1,0:T(8,128)(2,1)S(1)}, s32[36,1,128]{2,1,0:T(1,128)S(1)}, f32[10,256,256]{2,1,0:T(8,128)S(1)}) custom-call(s32[16]{0:T(128)S(1)} %copy-done.6, bf16[16,80,256]{2,1,0:T(8,128)(2,1)S(1)} %copy-done.2, bf16[16,32,256]{2,1,0:T(8,128)(2,1)S(1)} %copy-done.5, ...), custom_call_target="tpu_custom_call" | custom-call | tf_op jit(solution)/shard_map/pallas_call | solution.py:124
  9.8 1.4 %copy-done = bf16[36,256,80]{2,1,0:T(8,128)(2,1)} copy-done((bf16[36,256,80]{2,1,0:T(8,128)(2,1)}, bf16[36,256,80]{2,1,0:T(8,128)(2,1)S(1)}, u32[]{:S(2)}) %copy-start) | copy-done | bytes 1474584
  11.2 0.8 copy-done.3
  12.1 0.1 copy.11
  12.2 0.1 copy.12
  12.3 0.7 gather_fusion
  12.9 0.1 copy.13
  13.0 0.1 reshape.5
  13.1 0.8 clamp_add_fusion
  13.9 0.7 fusion.1.kind_ref
  14.6 1.7 %copy-done.1 = bf16[36,256,80]{2,1,0:T(8,128)(2,1)S(1)} copy-done((bf16[36,256,80]{2,1,0:T(8,128)(2,1)S(1)}, bf16[36,256,80]{2,1,0:T(8,128)(2,1)}, u32[]{:S(2)}) %copy-start.1) | copy-done | bytes 1474584
  16.2 1.1 %copy-done.4 = bf16[36,32,256]{2,1,0:T(8,128)(2,1)S(1)} copy-done((bf16[36,32,256]{2,1,0:T(8,128)(2,1)S(1)}, bf16[36,32,256]{2,1,0:T(8,128)(2,1)}, u32[]{:S(2)}) %copy-start.4) | copy-done | bytes 589848
  17.3 20.6 %shard_map.56 = (bf16[16,9,256,256]{3,2,1,0:T(8,128)(2,1)}, f32[16,32,256]{2,1,0:T(8,128)S(1)}, f32[32,32]{1,0:T(8,128)S(1)}) custom-call(s32[16,9]{1,0:T(8,128)S(1)} %get-tuple-element.26.slot_ref, s32[16,9]{1,0:T(8,128)S(1)} %fusion.1.kind_ref, bf16[36,256,80]{2,1,0:T(8,128)(2,1)S(1)} %copy-done.1, bf16[16,80,256]{2,1,0:T(8,128)(2,1)S(1)} %get-tuple-element.17.own_ref, ...), custom_call_target="tpu_custom_call" | custom-call | tf_op jit(solution)/shard_map/pallas_call | solution.py:374
  37.9 28.4 %shard_map.57.iter_ref = bf16[36,32,256]{2,1,0:T(8,128)(2,1)S(1)} custom-call(f32[32,32]{1,0:T(8,128)S(1)} %get-tuple-element.20.gram_ref, f32[16,32,256]{2,1,0:T(8,128)S(1)} %get-tuple-element.21.applied_ref), custom_call_target="tpu_custom_call" | custom-call | tf_op jit(solution)/shard_map/pallas_call | solution.py:321
  66.3 15.4 %shard_map.58 = (f32[16,32,256]{2,1,0:T(8,128)S(1)}, f32[32,32]{1,0:T(8,128)S(1)}) custom-call(s32[16,9]{1,0:T(8,128)S(1)} %get-tuple-element.26.slot_ref, bf16[36,32,256]{2,1,0:T(8,128)(2,1)S(1)} %shard_map.57.iter_ref, bf16[16,9,256,256]{3,2,1,0:T(8,128)(2,1)} %get-tuple-element.22.blocks_ref), custom_call_target="tpu_custom_call" | custom-call | tf_op jit(solution)/shard_map/pallas_call | solution.py:388
  81.8 16.7 %shard_map.59 = f32[16,32,256]{2,1,0:T(8,128)S(1)} custom-call(f32[32,32]{1,0:T(8,128)S(1)} %get-tuple-element.23.gram_ref, f32[16,32,256]{2,1,0:T(8,128)S(1)} %get-tuple-element.24.applied_ref), custom_call_target="tpu_custom_call" | custom-call | tf_op jit(solution)/shard_map/pallas_call | solution.py:321
  98.5 0.8 copy.15
  (8 shorter events, 0.0 us)
Async XLA Ops:
  1.6 1.1 %copy-start.2 = (bf16[16,80,256]{2,1,0:T(8,128)(2,1)S(1)}, bf16[16,80,256]{2,1,0:T(8,128)(2,1)}, u32[]{:S(2)}) copy-start(bf16[16,80,256]{2,1,0:T(8,128)(2,1)} %members_ref.1) | copy-start | bytes 1966084
  2.7 0.9 copy-start.5
  3.6 0.7 copy-start.6
  9.8 1.4 %copy-start = (bf16[36,256,80]{2,1,0:T(8,128)(2,1)}, bf16[36,256,80]{2,1,0:T(8,128)(2,1)S(1)}, u32[]{:S(2)}) copy-start(bf16[36,256,80]{2,1,0:T(8,128)(2,1)S(1)} %get-tuple-element.16.turned_ref) | copy-start | bytes 4423684
  11.2 0.8 copy-start.3
  14.6 1.7 %copy-start.1 = (bf16[36,256,80]{2,1,0:T(8,128)(2,1)S(1)}, bf16[36,256,80]{2,1,0:T(8,128)(2,1)}, u32[]{:S(2)}) copy-start(bf16[36,256,80]{2,1,0:T(8,128)(2,1)} %copy-done) | copy-start | bytes 4423684
  16.2 1.1 %copy-start.4 = (bf16[36,32,256]{2,1,0:T(8,128)(2,1)S(1)}, bf16[36,32,256]{2,1,0:T(8,128)(2,1)}, u32[]{:S(2)}) copy-start(bf16[36,32,256]{2,1,0:T(8,128)(2,1)} %copy-done.3) | copy-start | bytes 1769476

commit v4 on v3

--- a/solution.py
+++ b/solution.py
@@ -145,21 +145,18 @@
     )(wet_counts, members, initial, place)
 
 
-def gram_add(step, applied, gram_ref):
-    part = lax.dot_general(
-        applied, applied, (((1,), (1,)), ((), ())), precision=HIGH, preferred_element_type=jnp.float32
-    )
-
-    @pl.when(step == 0)
-    def _():
-        gram_ref[...] = part
-
-    @pl.when(step != 0)
-    def _():
-        gram_ref[...] += part
-
-
-def first_kernel(slot_ref, kind_ref, turned_ref, own_ref, iter_ref, table_ref, blocks_ref, applied_ref, gram_ref):
+def local_gram(applied_ref):
+    total = None
+    for a in range(applied_ref.shape[0]):
+        applied = applied_ref[a]
+        part = lax.dot_general(
+            applied, applied, (((1,), (1,)), ((), ())), precision=HIGH, preferred_element_type=jnp.float32
+        )
+        total = part if total is None else total + part
+    return total
+
+
+def first_kernel(slot_ref, kind_ref, turned_ref, own_ref, iter_ref, table_ref, blocks_ref, applied_ref):
     step = pl.program_id(0)
     own = own_ref[0]
     total = None
@@ -171,17 +168,15 @@
         part = jnp.dot(iter_ref[at], block, preferred_element_type=jnp.float32)
         total = part if total is None else total + part
     applied_ref[0] = total
-    gram_add(step, total, gram_ref)
-
-
-def later_kernel(slot_ref, iter_ref, blocks_ref, applied_ref, gram_ref):
+
+
+def later_kernel(slot_ref, iter_ref, blocks_ref, applied_ref):
     step = pl.program_id(0)
     total = None
     for s in range(slot_ref.shape[1]):
         part = jnp.dot(iter_ref[slot_ref[step, s]], blocks_ref[0, s], preferred_element_type=jnp.float32)
         total = part if total is None else total + part
     applied_ref[0] = total
-    gram_add(step, total, gram_ref)
 
 
 def device_at(index):
@@ -234,15 +229,15 @@
     work = jnp.concatenate([left, (rows == cols).astype(jnp.float32)], axis=1)
     down = lax.broadcasted_iota(jnp.int32, (rank, 1), 0)
     for j in range(rank):
-        root = lax.sqrt(work[j : j + 1, j : j + 1])
-        line = work[j : j + 1, :] / root
-        factor = work[:, j : j + 1] / root
-        work = jnp.where(down > j, work - factor * line, jnp.where(down == j, line, work))
-    return work[:, rank:]
+        column = jnp.broadcast_to(work[:, j : j + 1], work.shape)
+        line = work[j : j + 1, :] / column[j : j + 1, :]
+        work = jnp.where(down > j, work - column * line, work)
+    pivots = jnp.sum(jnp.where(rows == cols, work[:, :rank], 0.0), axis=1, keepdims=True)
+    return work[:, rank:] / lax.sqrt(pivots)
 
 
 def norm_kernel(
-    total_points, groups, edge, gram_ref, applied_ref, fresh_ref,
+    total_points, groups, edge, applied_ref, fresh_ref,
     source, inbox, halo, send_sem, recv_sem, halo_send, halo_recv,
 ):
     length = lax.axis_size(AXES)
@@ -263,7 +258,7 @@
         def _():
             pl.semaphore_signal(barrier, inc=1, device_id=device_at(me + by), device_id_type=mesh_ids)
 
-    source[0] = gram_ref[...]
+    source[0] = local_gram(applied_ref)
     if edge:
         greeted = greeted + jnp.minimum(me, 1) + jnp.minimum(length - 1 - me, 1)
     pl.semaphore_wait(barrier, greeted)
@@ -312,7 +307,7 @@
             fresh_ref[landing] = jnp.zeros(halo.shape[1:], halo.dtype)
 
 
-def normalise(gram, applied, total_points, edge, dtype, call_id):
+def normalise(applied, total_points, edge, dtype, call_id):
     tiles, rank, points = applied.shape
     groups = digit_groups(lax.axis_size(AXES))
     widest = max(size for _, size in groups)
@@ -320,7 +315,7 @@
     vmem = pl.BlockSpec(memory_space=pltpu.VMEM)
     return pl.pallas_call(
         functools.partial(norm_kernel, total_points, groups, edge),
-        in_specs=[vmem, vmem],
+        in_specs=[vmem],
         out_specs=vmem,
         out_shape=jax.ShapeDtypeStruct((tiles + 2 * edge, rank, points), dtype),
         scratch_shapes=[
@@ -335,7 +330,7 @@
         compiler_params=pltpu.CompilerParams(
             collective_id=call_id, has_side_effects=True, vmem_limit_bytes=40 * 1024 * 1024
         ),
-    )(gram, applied)
+    )(applied)
 
 
 def whole(shape):
@@ -369,28 +364,27 @@
     delta = jnp.clip(place[slot] - tile_coords[:, None, :], -1, 1) + 1
     kind = jnp.where(neighbours >= 0, delta[..., 0] * 3 + delta[..., 1], 9)
     applied_shape = jax.ShapeDtypeStruct((tiles, rank, points), jnp.float32)
-    gram_shape = jax.ShapeDtypeStruct((rank, rank), jnp.float32)
     blocks_shape = jax.ShapeDtypeStruct((tiles, slots, points, points), jnp.bfloat16)
-    blocks, applied, gram = pl.pallas_call(
+    blocks, applied = pl.pallas_call(
         first_kernel,
         grid=(tiles,),
         in_specs=[
             smem(), smem(), whole(turned.shape), per_tile(own_rows.shape), whole(current.shape), whole(table.shape),
         ],
-        out_specs=[per_tile(blocks_shape.shape), per_tile(applied_shape.shape), whole(gram_shape.shape)],
-        out_shape=[blocks_shape, applied_shape, gram_shape],
+        out_specs=[per_tile(blocks_shape.shape), per_tile(applied_shape.shape)],
+        out_shape=[blocks_shape, applied_shape],
         compiler_params=PARAMS,
     )(slot, kind, turned, own_rows, current, table)
     for sweep in range(ITERS):
         if sweep == ITERS - 1:
-            return normalise(gram, applied, total_points, 0, jnp.float32, sweep)
-        current = normalise(gram, applied, total_points, edge, jnp.bfloat16, sweep)
-        applied, gram = pl.pallas_call(
+            return normalise(applied, total_points, 0, jnp.float32, sweep)
+        current = normalise(applied, total_points, edge, jnp.bfloat16, sweep)
+        applied = pl.pallas_call(
             later_kernel,
             grid=(tiles,),
             in_specs=[smem(), whole(current.shape), per_tile(blocks.shape)],
-            out_specs=[per_tile(applied_shape.shape), whole(gram_shape.shape)],
-            out_shape=[applied_shape, gram_shape],
+            out_specs=per_tile(applied_shape.shape),
+            out_shape=applied_shape,
             compiler_params=PARAMS,
         )(slot, current, blocks)
 

time: 100 us -> 97.2 us (0.972)
  Pallas kernels: 86.7 us -> 84 us
    pallas_call x1, Pallas kernels: 15.4 us -> 13.8 us  [local(): pl.pallas_call(later_kernel, grid=(tiles,), in_specs=[smem(), whole(curre...]
    pallas_call x1, Pallas kernels: 20.6 us -> 19.5 us  [local(): pl.pallas_call(first_kernel, grid=(tiles,), in_specs=[smem(), smem(), who...]
where the time goes in v4:
time: 97.2 us; the launch traced here: 96.5 us
  Pallas kernels  84 us (86%)
  local copies, waits for them, and re-layouts  10.3 us (11%)
  other arithmetic  2.18 us (2%)
    pallas_call x2, Pallas kernels, normalise(): pl.pallas_call(functools.partial(norm_kernel, total_points, groups, edge)...  45 us
    pallas_call x1, Pallas kernels, local(): pl.pallas_call(first_kernel, grid=(tiles,), in_specs=[smem(), smem(), who...  19.5 us
    pallas_call x1, Pallas kernels, local(): pl.pallas_call(later_kernel, grid=(tiles,), in_specs=[smem(), whole(curre...  13.8 us
    unnamed x16, local copies, waits for them, and re-layouts  9.2 us
    pallas_call x1, Pallas kernels, opening(): pl.pallas_call(functools.partial(open_kernel, edge, 1.0 / (count - 1.0)),...  5.55 us

profile of v4, /device:TPU:0, one launch (start us, length us, event | category | flops | bytes accessed | tf_op | source)
XLA Modules:
  0.0 96.5 jit_solution(12653958711667429980)
XLA Ops:
  0.0 0.8 copy.10
  0.8 0.7 compare_select_fusion
  1.5 0.1 reshape.6
  1.6 0.0 copy-start.2
  1.6 1.1 %copy-done.2 = bf16[16,80,256]{2,1,0:T(8,128)(2,1)S(1)} copy-done((bf16[16,80,256]{2,1,0:T(8,128)(2,1)S(1)}, bf16[16,80,256]{2,1,0:T(8,128)(2,1)}, u32[]{:S(2)}) %copy-start.2) | copy-done | bytes 655384
  2.7 0.9 copy-done.5
  3.6 0.7 copy-done.6
  4.3 5.6 %shard_map.55 = (bf16[16,80,256]{2,1,0:T(8,128)(2,1)S(1)}, bf16[36,256,80]{2,1,0:T(8,128)(2,1)S(1)}, bf16[36,32,256]{2,1,0:T(8,128)(2,1)S(1)}, s32[36,1,128]{2,1,0:T(1,128)S(1)}, f32[10,256,256]{2,1,0:T(8,128)S(1)}) custom-call(s32[16]{0:T(128)S(1)} %copy-done.6, bf16[16,80,256]{2,1,0:T(8,128)(2,1)S(1)} %copy-done.2, bf16[16,32,256]{2,1,0:T(8,128)(2,1)S(1)} %copy-done.5, ...), custom_call_target="tpu_custom_call" | custom-call | tf_op jit(solution)/shard_map/pallas_call | solution.py:124
  9.8 1.4 %copy-done = bf16[36,256,80]{2,1,0:T(8,128)(2,1)} copy-done((bf16[36,256,80]{2,1,0:T(8,128)(2,1)}, bf16[36,256,80]{2,1,0:T(8,128)(2,1)S(1)}, u32[]{:S(2)}) %copy-start) | copy-done | bytes 1474584
  11.2 0.8 copy-done.3
  12.1 0.1 copy.11
  12.2 0.1 copy.12
  12.3 0.7 gather_fusion
  12.9 0.1 copy.13
  13.0 0.1 reshape.5
  13.1 0.8 clamp_add_fusion
  13.9 0.7 fusion.1.kind_ref
  14.6 1.7 %copy-done.1 = bf16[36,256,80]{2,1,0:T(8,128)(2,1)S(1)} copy-done((bf16[36,256,80]{2,1,0:T(8,128)(2,1)S(1)}, bf16[36,256,80]{2,1,0:T(8,128)(2,1)}, u32[]{:S(2)}) %copy-start.1) | copy-done | bytes 1474584
  16.2 1.1 %copy-done.4 = bf16[36,32,256]{2,1,0:T(8,128)(2,1)S(1)} copy-done((bf16[36,32,256]{2,1,0:T(8,128)(2,1)S(1)}, bf16[36,32,256]{2,1,0:T(8,128)(2,1)}, u32[]{:S(2)}) %copy-start.4) | copy-done | bytes 589848
  17.3 19.5 %shard_map.56 = (bf16[16,9,256,256]{3,2,1,0:T(8,128)(2,1)}, f32[16,32,256]{2,1,0:T(8,128)S(1)}) custom-call(s32[16,9]{1,0:T(8,128)S(1)} %get-tuple-element.20.slot_ref, s32[16,9]{1,0:T(8,128)S(1)} %fusion.1.kind_ref, bf16[36,256,80]{2,1,0:T(8,128)(2,1)S(1)} %copy-done.1, bf16[16,80,256]{2,1,0:T(8,128)(2,1)S(1)} %get-tuple-element.14.own_ref, ...), custom_call_target="tpu_custom_call" | custom-call | tf_op jit(solution)/shard_map/pallas_call | solution.py:368
  36.8 28.3 %shard_map.57.iter_ref = bf16[36,32,256]{2,1,0:T(8,128)(2,1)S(1)} custom-call(f32[16,32,256]{2,1,0:T(8,128)S(1)} %get-tuple-element.17.applied_ref), custom_call_target="tpu_custom_call" | custom-call | tf_op jit(solution)/shard_map/pallas_call | solution.py:316
  65.2 13.8 %shard_map.58.applied_ref = f32[16,32,256]{2,1,0:T(8,128)S(1)} custom-call(s32[16,9]{1,0:T(8,128)S(1)} %get-tuple-element.20.slot_ref, bf16[36,32,256]{2,1,0:T(8,128)(2,1)S(1)} %shard_map.57.iter_ref, bf16[16,9,256,256]{3,2,1,0:T(8,128)(2,1)} %get-tuple-element.18.blocks_ref), custom_call_target="tpu_custom_call" | custom-call | tf_op jit(solution)/shard_map/pallas_call | solution.py:382
  79.0 16.7 %shard_map.59 = f32[16,32,256]{2,1,0:T(8,128)S(1)} custom-call(f32[16,32,256]{2,1,0:T(8,128)S(1)} %shard_map.58.applied_ref), custom_call_target="tpu_custom_call" | custom-call | tf_op jit(solution)/shard_map/pallas_call | solution.py:316
  95.7 0.8 copy.15
  (8 shorter events, 0.0 us)
Async XLA Ops:
  1.6 1.1 %copy-start.2 = (bf16[16,80,256]{2,1,0:T(8,128)(2,1)S(1)}, bf16[16,80,256]{2,1,0:T(8,128)(2,1)}, u32[]{:S(2)}) copy-start(bf16[16,80,256]{2,1,0:T(8,128)(2,1)} %members_ref.1) | copy-start | bytes 1966084
  2.7 0.9 copy-start.5
  3.6 0.7 copy-start.6
  9.8 1.4 %copy-start = (bf16[36,256,80]{2,1,0:T(8,128)(2,1)}, bf16[36,256,80]{2,1,0:T(8,128)(2,1)S(1)}, u32[]{:S(2)}) copy-start(bf16[36,256,80]{2,1,0:T(8,128)(2,1)S(1)} %get-tuple-element.13.turned_ref) | copy-start | bytes 4423684
  11.2 0.8 copy-start.3
  14.6 1.7 %copy-start.1 = (bf16[36,256,80]{2,1,0:T(8,128)(2,1)S(1)}, bf16[36,256,80]{2,1,0:T(8,128)(2,1)}, u32[]{:S(2)}) copy-start(bf16[36,256,80]{2,1,0:T(8,128)(2,1)} %copy-done) | copy-start | bytes 4423684
  16.2 1.1 %copy-start.4 = (bf16[36,32,256]{2,1,0:T(8,128)(2,1)S(1)}, bf16[36,32,256]{2,1,0:T(8,128)(2,1)}, u32[]{:S(2)}) copy-start(bf16[36,32,256]{2,1,0:T(8,128)(2,1)} %copy-done.3) | copy-start | bytes 1769476
